TPU v7x, 128 devices: a whole 4x4x4 slice. The times are simulated.
128 devices in a mesh: group: 16 (over z, y), row: 4 (over x_lo, core), col: 2 (over x_hi).
Axes of the slice: x: 4 (x_hi: 2, x_lo: 2; x = x_hi * 2 + x_lo), y: 4, z: 4, core: 2. Of those that a mesh axis runs over, the one named last changes fastest.
Arguments:
- front_entries: bfloat16 [16, 20480, 512], P('group', 'row', 'col'), as said below
- contrib: bfloat16 [16, 4, 2, 16, 4, 8, 128, 128], P('group', 'row', 'col'), may hold values from -6 to 6
- counts: int32 [16, 4, 2, 16, 4], P('group', 'row', 'col'), may hold values from 0 to 8, as said below
- tile_rows: int32 [16, 4, 2, 16, 4, 8], P('group', 'row', 'col'), may hold values from 0 to 39, as said below
- tile_cols: int32 [16, 4, 2, 16, 4, 8], P('group', 'row', 'col'), may hold values from 0 to 1
Outputs:
- factored: float32 [16, 20480, 512], P('group', 'row', 'col')
Inputs may be any that keep to these rules, and one draw needn't show every extreme that they name: `counts`: slots at or past the count carry nothing; in every draw some owner of some front has 8 live slots from every source, and some fronts receive 8 // 2 or more from every source. `tile_rows`: row tile within the owner's 40 tiles; for grid row 0 never one of the first 2 tiles. `front_entries`: the leading 2 * 128 rows and columns of every front hold a symmetric-part positive definite block.
All inputs are finite; a program needn't handle non-finite values.
Results may differ from a plain program's by a relative error of at most 0.0017.
Values may be sent and summed in bfloat16 or wider, within the bound.
No kernel may reach another device: no remote copies, remote signals or barrier semaphores. Data moves between devices by JAX's collectives and lax.ppermute only.
A program may use at most 128 MiB of HBM per device.

v0:
```python
import jax
import jax.numpy as jnp
from jax import lax
from jax.sharding import PartitionSpec as P

NPANEL = 2


def spread(x, axis, root):
    mine = lax.axis_index(axis) == root
    return lax.psum(jnp.where(mine, x, jnp.zeros_like(x)), axis)


def local(front_entries, contrib, counts, tile_rows, tile_cols):
    frontal = front_entries[0].astype(jnp.float32)
    local_rows, local_cols = frontal.shape
    fronts = contrib.shape[3]
    grid_rows = contrib.shape[4]
    slot_count = contrib.shape[5]
    panel_width = contrib.shape[6]
    outgoing = contrib.reshape(fronts, grid_rows, slot_count, panel_width, panel_width)
    received = lax.all_to_all(
        outgoing.reshape(fronts * grid_rows, slot_count, panel_width, panel_width),
        ("group", "row"),
        split_axis=0,
        concat_axis=0,
        tiled=True,
    )
    sources = fronts * grid_rows * slot_count
    received = received.reshape(sources, panel_width * panel_width)
    row_tiles = local_rows // panel_width
    col_tiles = local_cols // panel_width
    live_slots = (
        jnp.arange(slot_count, dtype=jnp.int32)[None, :]
        < counts.reshape(fronts * grid_rows)[:, None]
    ).reshape(sources)
    targets = tile_rows.reshape(sources) * col_tiles + tile_cols.reshape(sources)
    onehot = (
        (jnp.arange(row_tiles * col_tiles, dtype=jnp.int32)[:, None] == targets[None, :])
        & live_slots[None, :]
    ).astype(jnp.bfloat16)
    assembled = jnp.dot(onehot, received, preferred_element_type=jnp.float32)
    assembled = (
        assembled.reshape(row_tiles, col_tiles, panel_width, panel_width)
        .transpose(0, 2, 1, 3)
        .reshape(local_rows, local_cols)
    )
    frontal = frontal + assembled
    row_position = lax.axis_index("row")
    column_position = lax.axis_index("col")
    global_row = row_position * local_rows + jnp.arange(local_rows, dtype=jnp.int32)[:, None]
    global_col = column_position * local_cols + jnp.arange(local_cols, dtype=jnp.int32)[None, :]
    for panel_index in range(NPANEL):
        start_col = panel_index * panel_width
        stop_col = start_col + panel_width
        panel_cols = frontal[:, start_col:stop_col]
        own_factor = jnp.linalg.cholesky(panel_cols[start_col:stop_col])
        factor = spread(own_factor, "row", 0)
        solved = jax.scipy.linalg.solve_triangular(factor, panel_cols.T, lower=True).T
        candidate = solved.at[start_col:stop_col].set(own_factor)
        in_block = (global_row >= start_col) & (global_row < stop_col)
        lpanel = jnp.where(global_row < start_col, 0.0, jnp.where(in_block, candidate, solved))
        panel_half = lpanel.astype(jnp.bfloat16)
        panel_local = spread(panel_half, "col", 0)
        column_piece = lax.dynamic_slice_in_dim(
            panel_local, column_position * local_cols, local_cols, 0
        )
        column_part = spread(column_piece, "row", 0)
        update = jnp.einsum(
            "ik,jk->ij", panel_local, column_part, preferred_element_type=jnp.float32
        )
        frontal = jnp.where(global_col >= stop_col, frontal - update, frontal)
        frontal = frontal.at[:, start_col:stop_col].set(
            jnp.where(column_position == 0, lpanel, frontal[:, start_col:stop_col])
        )
    return frontal[None]


def solution(mesh):
    placed = (
        P("group", "row", "col"),
        P("group", "row", "col", None, None, None, None, None),
        P("group", "row", "col", None, None),
        P("group", "row", "col", None, None, None),
        P("group", "row", "col", None, None, None),
    )
    return jax.shard_map(
        local, mesh=mesh, in_specs=placed, out_specs=P("group", "row", "col"), check_vma=False
    )
```

profile of v0, /device:TPU:14, one launch (start us, length us, event | category | flops | bytes accessed | tf_op | source)
XLA Modules:
  0.0 683.0 jit_solution(18158952502725827502)
XLA Ops:
  6.5 10.2 %all-to-all-start = ((bf16[64,8,128,128]{3,2,1,0:T(8,128)(2,1)}), bf16[64,8,128,128]{3,2,1,0:T(8,128)(2,1)}, u32[]{:S(2)}, u32[]{:S(2)}) async-start(bf16[64,8,128,128]{3,2,1,0:T(8,128)(2,1)} %bitcast.80), calls=%async_computation | async-start | bytes 33554432 | tf_op jit(solution)/shard_map/all_to_all | solution.py:22
  16.9 0.1 add.95
  17.3 0.1 lt.69
  17.4 3.0 copy.19
  20.4 234.7 %all-to-all-done = bf16[64,8,128,128]{3,2,1,0:T(8,128)(2,1)} async-done(((bf16[64,8,128,128]{3,2,1,0:T(8,128)(2,1)}), bf16[64,8,128,128]{3,2,1,0:T(8,128)(2,1)}, u32[]{:S(2)}, u32[]{:S(2)}) %all-to-all-start) | async-done | bytes 16777248 | tf_op jit(solution)/shard_map/all_to_all | solution.py:22
  255.1 19.3 %copy.42 = bf16[64,8,128,128]{3,1,2,0:T(8,128)(2,1)} copy(bf16[64,8,128,128]{3,2,1,0:T(8,128)(2,1)} %all-to-all-done) | data formatting | bytes 33554432
  274.4 22.5 %copy.22 = bf16[16384,512]{1,0:T(8,128)(2,1)} copy(bf16[16384,512]{0,1:T(8,128)(2,1)} %bitcast.75) | data formatting | bytes 33554432 | tf_op jit(solution)/shard_map/dot_general | solution.py:42
  296.9 11.1 %convolution_bitcast_fusion = f32[40,128,2,128]{3,0,1,2:T(8,128)} fusion(bf16[128,128,512,1]{2,1,0,3:T(8,128)(2,1)} %bitcast.74, s32[512]{0:T(512)S(1)} %add.95, s32[40,2]{0,1:T(2,128)S(1)} %multiply_add_fusion.1, pred[512]{0:T(512)(128)(4,1)S(1)} %lt.69), kind=kOutput, calls=%fused_computation.15 | convolution fusion | flops 1342259200 | bytes 22022976 | tf_op jit(solution)/shard_map/dot_general | solution.py:42
  308.0 6.3 copy.23
  314.3 4.0 bitcast_add_fusion
  318.3 2.3 copy-done.1
  320.6 0.1 copy.24
  320.7 0.9 fusion.16
  321.6 11.7 %cholesky.44 = f32[128,128]{1,0:T(8,128)S(1)} custom-call(f32[128,128]{1,0:T(8,128)S(1)} %fusion.16), custom_call_target="Cholesky" | custom-call | tf_op jit(solution)/shard_map/jit(cholesky)/cholesky | solution.py:57
  333.3 0.6 compare_reduce_fusion.1
  334.0 1.2 fusion.18
  335.2 0.2 all-reduce.9.cloned.1.call-start
  335.4 50.1 %all-reduce.7.cloned.1.call-done = f32[128,128]{1,0:T(8,128)} async-done(((f32[128,128]{1,0:T(8,128)}), f32[128,128]{1,0:T(8,128)}) %all-reduce.7.cloned.1.call-update) | async-done | bytes 65552 | tf_op jit(solution)/shard_map/psum | solution.py:11
  385.5 0.8 select_bitcast_fusion.1
  386.4 9.8 %custom-call.6 = f32[1,128,128]{1,2,0:T(8,128)S(1)} custom-call(f32[1,128,128]{2,1,0:T(8,128)S(1)} %select_bitcast_fusion.1), custom_call_target="InvertDiagBlocksLowerTriangular" | custom-call | tf_op jit(solution)/shard_map/jit(_solve_triangular)/triangular_solve | solution.py:59
  396.2 4.1 fusion.4
  400.4 0.6 bitcast_select_fusion.1
  401.1 1.4 fusion.5
  402.6 0.6 compare_reduce_fusion.2
  403.2 53.4 %all-reduce.9.cloned.1.call-done = bf16[5120,128]{0,1:T(8,128)(2,1)} async-done(((bf16[5120,128]{0,1:T(8,128)(2,1)}), bf16[5120,128]{0,1:T(8,128)(2,1)}) %all-reduce.9.cloned.1.call-update) | async-done | bytes 1310736 | tf_op jit(solution)/shard_map/psum | solution.py:11
  456.6 1.5 dynamic-slice_select_fusion.1
  458.2 36.6 %all-reduce.11.cloned.1.call-done = bf16[256,128]{0,1:T(8,128)(2,1)} async-done(((bf16[256,128]{0,1:T(8,128)(2,1)}), bf16[256,128]{0,1:T(8,128)(2,1)}) %all-reduce.11.cloned.1.call-update) | async-done | bytes 65552 | tf_op jit(solution)/shard_map/psum | solution.py:11
  494.7 3.8 subtract_select_fusion.1
  498.6 1.2 fusion
  499.8 2.3 copy-done
  502.3 0.9 fusion.14
  503.1 11.7 %cholesky.55 = f32[128,128]{1,0:T(8,128)S(1)} custom-call(f32[128,128]{1,0:T(8,128)S(1)} %fusion.14), custom_call_target="Cholesky" | custom-call | tf_op jit(solution)/shard_map/jit(cholesky)/cholesky | solution.py:57
  514.9 0.6 compare_reduce_fusion
  515.5 1.2 fusion.19
  516.7 0.3 all-reduce.15.cloned.1.call-start
  517.0 36.1 %all-reduce.13.cloned.1.call-done = f32[128,128]{1,0:T(8,128)} async-done(((f32[128,128]{1,0:T(8,128)}), f32[128,128]{1,0:T(8,128)}) %all-reduce.13.cloned.1.call-update) | async-done | bytes 65552 | tf_op jit(solution)/shard_map/psum | solution.py:11
  553.1 0.8 select_bitcast_fusion
  553.9 9.8 %custom-call.7 = f32[1,128,128]{1,2,0:T(8,128)S(1)} custom-call(f32[1,128,128]{2,1,0:T(8,128)S(1)} %select_bitcast_fusion), custom_call_target="InvertDiagBlocksLowerTriangular" | custom-call | tf_op jit(solution)/shard_map/jit(_solve_triangular)/triangular_solve | solution.py:59
  563.7 4.1 fusion.3
  568.0 0.6 bitcast_select_fusion
  568.7 1.4 fusion.6
  570.1 54.0 %all-reduce.15.cloned.1.call-done = bf16[5120,128]{0,1:T(8,128)(2,1)} async-done(((bf16[5120,128]{0,1:T(8,128)(2,1)}), bf16[5120,128]{0,1:T(8,128)(2,1)}) %all-reduce.15.cloned.1.call-update) | async-done | bytes 1310736 | tf_op jit(solution)/shard_map/psum | solution.py:11
  624.2 1.5 dynamic-slice_select_fusion
  625.7 36.6 %all-reduce.17.cloned.1.call-done = bf16[256,128]{0,1:T(8,128)(2,1)} async-done(((bf16[256,128]{0,1:T(8,128)(2,1)}), bf16[256,128]{0,1:T(8,128)(2,1)}) %all-reduce.17.cloned.1.call-update) | async-done | bytes 65552 | tf_op jit(solution)/shard_map/psum | solution.py:11
  662.3 3.8 subtract_select_fusion
  666.1 2.3 copy.52
  668.4 1.9 fusion.2
  670.3 5.9 copy.32
  (43 shorter events, 1.2 us)
Async XLA Ops:
  6.5 10.2 %copy-start.2 = (s32[1,1,1,16,4,8]{3,5,4,2,1,0:T(8,128)S(1)}, s32[1,1,1,16,4,8]{3,5,4,2,1,0:T(8,128)}, u32[]{:S(2)}) copy-start(s32[1,1,1,16,4,8]{3,5,4,2,1,0:T(8,128)} %param.20) | copy-start | bytes 6148
  6.5 10.3 %copy-start.3 = (s32[1,1,1,16,4,8]{3,5,4,2,1,0:T(8,128)S(1)}, s32[1,1,1,16,4,8]{3,5,4,2,1,0:T(8,128)}, u32[]{:S(2)}) copy-start(s32[1,1,1,16,4,8]{3,5,4,2,1,0:T(8,128)} %param.19) | copy-start | bytes 6148
  6.5 10.5 %copy-start.4 = (s32[1,1,1,16,4]{3,4,2,1,0:T(4,128)S(1)}, s32[1,1,1,16,4]{3,4,2,1,0:T(4,128)}, u32[]{:S(2)}) copy-start(s32[1,1,1,16,4]{3,4,2,1,0:T(4,128)} %param.18) | copy-start | bytes 772
  6.5 248.6 %all-to-all-start = ((bf16[64,8,128,128]{3,2,1,0:T(8,128)(2,1)}), bf16[64,8,128,128]{3,2,1,0:T(8,128)(2,1)}, u32[]{:S(2)}, u32[]{:S(2)}) async-start(bf16[64,8,128,128]{3,2,1,0:T(8,128)(2,1)} %bitcast.80), calls=%async_computation | async-start | bytes 33554432 | tf_op jit(solution)/shard_map/all_to_all | solution.py:22
  16.7 368.8 %all-reduce.7.cloned.1.call-start = ((), (), s32[]{:S(2)}) async-start(), calls=%async_computation.1 | async-start | bytes 131072 | tf_op jit(solution)/shard_map/psum | solution.py:11
  318.2 2.4 copy-start.1
  335.2 121.4 %all-reduce.9.cloned.1.call-start = ((), (), s32[]{:S(2)}) async-start(), calls=%async_computation.2 | async-start | bytes 2621440 | tf_op jit(solution)/shard_map/psum | solution.py:11
  402.5 92.2 %all-reduce.11.cloned.1.call-start = ((), (), s32[]{:S(2)}) async-start(), calls=%async_computation.3 | async-start | bytes 131072 | tf_op jit(solution)/shard_map/psum | solution.py:11
  458.1 95.0 %all-reduce.13.cloned.1.call-start = ((), (), s32[]{:S(2)}) async-start(), calls=%async_computation.4 | async-start | bytes 131072 | tf_op jit(solution)/shard_map/psum | solution.py:11
  499.8 2.4 copy-start
  516.7 107.4 %all-reduce.15.cloned.1.call-start = ((), (), s32[]{:S(2)}) async-start(), calls=%async_computation.5 | async-start | bytes 2621440 | tf_op jit(solution)/shard_map/psum | solution.py:11
  570.1 92.2 %all-reduce.17.cloned.1.call-start = ((), (), s32[]{:S(2)}) async-start(), calls=%async_computation.6 | async-start | bytes 131072 | tf_op jit(solution)/shard_map/psum | solution.py:11
Sparse Core Ops, SparseCore 0:
  335.3 50.1 all-reduce.6
  402.7 53.9 all-reduce.8
  459.1 35.6 all-reduce.10
  516.8 36.2 all-reduce.12
  570.2 53.8 all-reduce.14
  626.6 35.5 all-reduce.16
where the time goes:
time: 687 us; the launch traced here: 683 us
  waiting for transfers between devices  502 us (73%)
  local copies, waits for them, and re-layouts  65 us (9%)
  other arithmetic  65 us (9%)
  matrix products  26.9 us (4%)
  between operations  13.8 us (2%)
  starting transfers between devices  10.8 us (2%)
    psum x6, waiting for transfers between devices, spread(): return lax.psum(jnp.where(mine, x, jnp.zeros_like(x)), axis)  267 us
    all_to_all x1, waiting for transfers between devices, local(): lax.all_to_all(outgoing.reshape(fronts * grid_rows, slot_count, panel_wid...  235 us
    unnamed x16, local copies, waits for them, and re-layouts  29.6 us
    another operation x6, other arithmetic, local(): own_factor = jnp.linalg.cholesky(panel_cols[start_col:stop_col])  24.8 us
    dot_general x1, local copies, waits for them, and re-layouts, local(): assembled = jnp.dot(onehot, received, preferred_element_type=jnp.float32)  22.5 us
    another operation x4, other arithmetic, local(): jax.scipy.linalg.solve_triangular(factor, panel_cols.T, lower=True)  21.3 us
  transfers between devices with their start and end apart: 7, of which 7 were waited for; matrix products, arithmetic and copies ran while one was open for 1% of the time, Pallas kernels for 0%

commit v1 on v0

v1 whole, which is shorter than its diff:
```python
import functools

import jax
import jax.numpy as jnp
from jax import lax
from jax.experimental import pallas as pl
from jax.experimental.pallas import tpu as pltpu
from jax.sharding import PartitionSpec as P

PB = 128
CHUNKS = (32, 48, 32, 16)
CHAINS = 4
EXACT = lax.Precision.HIGHEST
VMEM = pl.BlockSpec(memory_space=pltpu.VMEM)


def dot_t(a, b):
    return lax.dot_general(a, b, (((1,), (1,)), ((), ())), preferred_element_type=jnp.float32)


def assemble_kernel(
    rows, tiles, block, target, place, x_ref, e_ref, t1_ref, t2_ref, l21_ref, l11_ref, l22_ref,
    f_ref, h_ref, *acc
):
    step = pl.program_id(0)

    @pl.when(step == 0)
    def _():
        for a in acc:
            a[...] = jnp.zeros_like(a)

    def add(i, carry):
        for j, a in enumerate(acc):
            slot = i * CHAINS + j
            where = pl.ds(pl.multiple_of(target[step * block + slot] * rows, rows), rows)
            a[where, :] += x_ref[slot].astype(jnp.float32)
        return carry

    lax.fori_loop(0, block // CHAINS, add, 0, unroll=4)

    @pl.when(step == pl.num_programs(0) - 1)
    def _():
        batch = 8
        span = batch * rows
        for g in range(tiles // batch):
            parts = []
            for c in range(2):
                here = slice((c * tiles + g * batch) * rows, (c * tiles + g * batch) * rows + span)
                total = acc[0][here, :]
                for a in acc[1:]:
                    total += a[here, :]
                entries = e_ref[g * batch : (g + 1) * batch, :, c * PB : (c + 1) * PB]
                parts.append(total + entries.astype(jnp.float32).reshape(span, PB))
            left, right = parts
            out = slice(g * batch, (g + 1) * batch)

            @pl.when(place[1] == 1)
            def _():
                f_ref[out, :, :PB] = left.reshape(batch, rows, PB)
                f_ref[out, :, PB:] = right.reshape(batch, rows, PB)

            @pl.when(place[1] == 0)
            def _():
                x1 = jnp.dot(left, t1_ref[...], precision=EXACT, preferred_element_type=jnp.float32)
                if g == 0:
                    top = jnp.concatenate([l11_ref[...], x1[rows:]], axis=0)
                    x1 = jnp.where(place[0] == 0, top, x1)
                h1 = x1.astype(jnp.bfloat16)
                right2 = right - dot_t(h1, l21_ref[...])
                x2 = jnp.dot(right2, t2_ref[...], precision=EXACT, preferred_element_type=jnp.float32)
                if g == 0:
                    top = jnp.concatenate([jnp.zeros((rows, PB), jnp.float32), l22_ref[...], x2[2 * rows :]], axis=0)
                    x2 = jnp.where(place[0] == 0, top, x2)
                f_ref[out, :, :PB] = x1.reshape(batch, rows, PB)
                f_ref[out, :, PB:] = x2.reshape(batch, rows, PB)
                h_ref[g * span : (g + 1) * span, :PB] = h1
                h_ref[g * span : (g + 1) * span, PB:] = x2.astype(jnp.bfloat16)


def assemble(target, place, received, entries, t1, t2, l21, l11, l22):
    slots, rows, _ = received.shape
    tiles = entries.shape[0]
    block = 64
    whole = lambda shape: pl.BlockSpec(shape, lambda i, *_: (0,) * len(shape))
    return pl.pallas_call(
        functools.partial(assemble_kernel, rows, tiles, block),
        grid_spec=pltpu.PrefetchScalarGridSpec(
            num_scalar_prefetch=2,
            grid=(slots // block,),
            in_specs=[
                pl.BlockSpec((block, rows, PB), lambda i, *_: (i, 0, 0)),
                whole(entries.shape),
                whole((PB, PB)),
                whole((PB, PB)),
                whole((PB, PB)),
                whole((rows, PB)),
                whole((rows, PB)),
            ],
            out_specs=[whole((tiles, rows, 2 * PB)), whole((tiles * rows, 2 * PB))],
            scratch_shapes=[pltpu.VMEM(((2 * tiles + 1) * rows, PB), jnp.float32)] * CHAINS,
        ),
        out_shape=[
            jax.ShapeDtypeStruct((tiles, rows, 2 * PB), jnp.float32),
            jax.ShapeDtypeStruct((tiles * rows, 2 * PB), jnp.bfloat16),
        ],
        compiler_params=pltpu.CompilerParams(
            dimension_semantics=("arbitrary",), vmem_limit_bytes=40 * 1024 * 1024
        ),
        cost_estimate=pl.CostEstimate(
            flops=slots * rows * PB * 40, bytes_accessed=slots * rows * PB * 2, transcendentals=0
        ),
        name="assemble",
    )(target, place, received, entries, t1, t2, l21, l11, l22)


def update_kernel(chunks, place, *refs):
    n = len(chunks)
    fronts, halves, p_ref, out_ref = refs[:n], refs[n : 2 * n], refs[2 * n], refs[2 * n + 1]
    start = 0
    for rows, f_ref, h_ref in zip(chunks, fronts, halves):
        here = slice(start, start + rows)

        @pl.when(place[1] == 0)
        def _():
            out_ref[:, here, :] = f_ref[...]

        @pl.when(place[1] == 1)
        def _():
            change = dot_t(h_ref[...], p_ref[...])
            out_ref[:, here, :] = f_ref[...] - change.reshape(f_ref.shape)

        start += rows


def update(place, fronts, halves, columns):
    tiles = fronts[0].shape[0]
    batch = 8
    chunks = tuple(f.shape[1] for f in fronts)
    return pl.pallas_call(
        functools.partial(update_kernel, chunks),
        grid_spec=pltpu.PrefetchScalarGridSpec(
            num_scalar_prefetch=1,
            grid=(tiles // batch,),
            in_specs=[pl.BlockSpec((batch, r, 2 * PB), lambda i, *_: (i, 0, 0)) for r in chunks]
            + [pl.BlockSpec((batch * r, 2 * PB), lambda i, *_: (i, 0)) for r in chunks]
            + [pl.BlockSpec((2 * PB, 2 * PB), lambda i, *_: (0, 0))],
            out_specs=pl.BlockSpec((batch, PB, 2 * PB), lambda i, *_: (i, 0, 0)),
        ),
        out_shape=jax.ShapeDtypeStruct((tiles, PB, 2 * PB), jnp.float32),
        compiler_params=pltpu.CompilerParams(
            dimension_semantics=("arbitrary",), vmem_limit_bytes=40 * 1024 * 1024
        ),
        name="update",
    )(place, *fronts, *halves, columns)


def from_first(x, axes, targets, own):
    total = own
    for t in targets:
        total = total + lax.ppermute(x, axes, [(0, t)])
    return total


def after(x, other):
    return lax.optimization_barrier((x, other))[0]


def inverse_t(factor):
    eye = jnp.eye(PB, dtype=jnp.float32)
    return jax.scipy.linalg.solve_triangular(factor, eye, lower=True).T


def local(front_entries, contrib, counts, tile_rows, tile_cols):
    entries = front_entries[0]
    row, col = lax.axis_index("row"), lax.axis_index("col")
    place = jnp.stack([row, col]).astype(jnp.int32)
    tiles = entries.shape[0] // PB
    owners = contrib.shape[3] * contrib.shape[4]
    slots = contrib.shape[5]
    outgoing = contrib.reshape(owners, slots, PB, PB)
    live = jnp.arange(slots, dtype=jnp.int32)[None, :] < counts.reshape(owners)[:, None]
    target = tile_cols.reshape(owners, slots) * tiles + tile_rows.reshape(owners, slots)
    target = jnp.where(live, target, 2 * tiles).reshape(owners * slots)

    lead = entries[: 2 * PB]
    lead = from_first(
        lead, "row", (1, 2, 3), jnp.where(row == 0, lead, jnp.zeros_like(lead))
    ).astype(jnp.float32)
    l11 = jnp.linalg.cholesky(lead[:PB, :PB])
    t1 = inverse_t(l11)
    l21 = jnp.dot(lead[PB:, :PB], t1, precision=EXACT).astype(jnp.bfloat16)
    rest = lead[PB:, PB:] - dot_t(l21, l21)
    l22 = jnp.linalg.cholesky(rest)
    t2 = inverse_t(l22)

    shaped = entries.reshape(tiles, PB, 2 * PB)
    fronts, halves, columns = [], [], []
    received, starts = [], []
    start = 0
    for k, rows in enumerate(CHUNKS):
        stop = start + rows
        starts.append(start)
        source = outgoing
        if k >= 1:
            source = after(source, received[k - 2] if k >= 2 else piece)
        piece = source[:, :, start:stop]
        if k >= 1:
            piece = after(piece, received[k - 1])
        if k >= 2:
            piece = after(piece, halves[k - 2])
        received.append(
            lax.all_to_all(
                piece, ("group", "row"), split_axis=0, concat_axis=0, tiled=True
            ).reshape(owners * slots, rows, PB)
        )
        f, h = assemble(
            target, place, received[k], shaped[:, start:stop], t1, t2, l21, l11[start:stop], l22[start:stop]
        )
        fronts.append(f)
        halves.append(lax.ppermute(h, "col", [(0, 1)]))
        columns.append(h[2 * rows : 4 * rows].reshape(2, rows, 2 * PB))
        start = stop
    last = len(CHUNKS) - 1
    parts = []
    for which in (range(last), (last,)):
        mine = [halves[k][2 * CHUNKS[k] : 4 * CHUNKS[k]].reshape(2, CHUNKS[k], 2 * PB) for k in which]
        mine = jnp.concatenate(mine, axis=1)
        sent = jnp.concatenate([columns[k] for k in which], axis=1)
        parts.append(
            from_first(sent, ("row", "col"), (3, 5, 7), jnp.where(row == 0, mine, jnp.zeros_like(mine)))
        )
    columns = jnp.concatenate(parts, axis=1).reshape(2 * PB, 2 * PB)
    return update(place, fronts, halves, columns).reshape(front_entries.shape)


def solution(mesh):
    placed = (
        P("group", "row", "col"),
        P("group", "row", "col", None, None, None, None, None),
        P("group", "row", "col", None, None),
        P("group", "row", "col", None, None, None),
        P("group", "row", "col", None, None, None),
    )
    return jax.shard_map(
        local, mesh=mesh, in_specs=placed, out_specs=P("group", "row", "col"), check_vma=False
    )
```

time: 687 us -> 387 us (0.56)
  waiting for transfers between devices: 502 us -> 210 us
  starting transfers between devices: 10.8 us -> 54.4 us
  Pallas kernels: 0 us -> 30.7 us
  local copies, waits for them, and re-layouts: 65 us -> 37.7 us
  matrix products: 26.9 us -> 0.92 us
  other arithmetic: 65 us -> 47.1 us
  between operations: 13.8 us -> 0.52 us
    psum x6 -> x0, waiting for transfers between devices: 267 us -> none  [spread(): return lax.psum(jnp.where(mine, x, jnp.zeros_like(x)), axis)]
    all_to_all x1 -> x4, waiting for transfers between devices: 235 us -> 98.2 us  [local(): lax.all_to_all(piece, ('group', 'row'), split_axis=0, concat_axis=0, tile...]
    ppermute x0 -> x13, waiting for transfers between devices: none -> 112 us  [the longest x9 74.5 us: from_first(): total = total + lax.ppermute(x, axes, [(0, t)])]
    pallas_call x0 -> x5, Pallas kernels: none -> 30.7 us  [the longest x4 23.3 us: assemble(): pl.pallas_call(functools.partial(assemble_kernel, rows, tiles, block), gr...]
    all_to_all x1 -> x4, starting transfers between devices: 10.2 us -> 40.5 us  [local(): lax.all_to_all(piece, ('group', 'row'), split_axis=0, concat_axis=0, tile...]
    slice x4 -> x25, local copies, waits for them, and re-layouts: 0.19 us -> 28.1 us  [the longest x4 22.2 us: local(): piece = source[:, :, start:stop]]
    dot_general x1 -> x0, local copies, waits for them, and re-layouts: 22.5 us -> none  [local(): assembled = jnp.dot(onehot, received, preferred_element_type=jnp.float32)]
    unnamed x16 -> x34, local copies, waits for them, and re-layouts: 29.6 us -> 9.01 us
  transfers between devices with their start and end apart: 7 -> 17, of which waited for: 7 -> 9; matrix products, arithmetic and copies ran while one was open for 1% -> 19% of each run, Pallas kernels for 0% -> 6%
where the time goes in v1:
time: 387 us; the launch traced here: 381 us
  waiting for transfers between devices  210 us (54%)
  starting transfers between devices  54.4 us (14%)
  other arithmetic  47.1 us (12%)
  local copies, waits for them, and re-layouts  37.7 us (10%)
  Pallas kernels  30.7 us (8%)
    all_to_all x4, waiting for transfers between devices, local(): lax.all_to_all(piece, ('group', 'row'), split_axis=0, concat_axis=0, tile...  98.2 us
    ppermute x9, waiting for transfers between devices, from_first(): total = total + lax.ppermute(x, axes, [(0, t)])  74.5 us
    all_to_all x4, starting transfers between devices, local(): lax.all_to_all(piece, ('group', 'row'), split_axis=0, concat_axis=0, tile...  40.5 us
    ppermute x4, waiting for transfers between devices, local(): halves.append(lax.ppermute(h, 'col', [(0, 1)]))  37.2 us
    pallas_call x4, Pallas kernels, assemble(): pl.pallas_call(functools.partial(assemble_kernel, rows, tiles, block), gr...  23.3 us
    slice x4, local copies, waits for them, and re-layouts, local(): piece = source[:, :, start:stop]  22.2 us
    another operation x4, other arithmetic, inverse_t(): return jax.scipy.linalg.solve_triangular(factor, eye, lower=True).T  21.1 us
    another operation x3, other arithmetic, local(): l11 = jnp.linalg.cholesky(lead[:PB, :PB])  12.4 us
  transfers between devices with their start and end apart: 17, of which 9 were waited for; matrix products, arithmetic and copies ran while one was open for 19% of the time, Pallas kernels for 6%

profile of v1, /device:TPU:14, one launch (start us, length us, event | category | flops | bytes accessed | tf_op | source)
XLA Modules:
  0.0 381.3 jit_solution(4529396686586719204)
XLA Ops:
  0.0 5.6 %slice.124 = bf16[64,8,32,128]{3,2,1,0:T(8,128)(2,1)} slice(bf16[64,8,128,128]{3,2,1,0:T(8,128)(2,1)} %bitcast.55), slice={[0:64], [0:8], [0:32], [0:128]} | slice | bytes 8388608 | tf_op jit(solution)/shard_map/slice | solution.py:206
  5.6 10.0 %all-to-all-start = ((bf16[64,8,32,128]{3,2,1,0:T(8,128)(2,1)}), bf16[64,8,32,128]{3,2,1,0:T(8,128)(2,1)}, u32[]{:S(2)}, u32[]{:S(2)}) async-start(bf16[64,8,32,128]{3,2,1,0:T(8,128)(2,1)} %slice.124), calls=%async_computation | async-start | bytes 8388608 | tf_op jit(solution)/shard_map/all_to_all | solution.py:212
  15.6 7.5 %slice.104 = bf16[64,8,48,128]{3,2,1,0:T(8,128)(2,1)} slice(bf16[64,8,128,128]{3,2,1,0:T(8,128)(2,1)} %bitcast.56), slice={[0:64], [0:8], [32:80], [0:128]} | slice | bytes 12582912 | tf_op jit(solution)/shard_map/slice | solution.py:206
  23.1 47.5 %all-to-all-done = bf16[64,8,32,128]{3,2,1,0:T(8,128)(2,1)} async-done(((bf16[64,8,32,128]{3,2,1,0:T(8,128)(2,1)}), bf16[64,8,32,128]{3,2,1,0:T(8,128)(2,1)}, u32[]{:S(2)}, u32[]{:S(2)}) %all-to-all-start) | async-done | bytes 4194336 | tf_op jit(solution)/shard_map/all_to_all | solution.py:212
  70.6 8.9 %all-to-all-start.1 = ((bf16[64,8,48,128]{3,2,1,0:T(8,128)(2,1)}), bf16[64,8,48,128]{3,2,1,0:T(8,128)(2,1)}, u32[]{:S(2)}, u32[]{:S(2)}) async-start(bf16[64,8,48,128]{3,2,1,0:T(8,128)(2,1)} %slice.104), calls=%async_computation.1 | async-start | bytes 12582912 | tf_op jit(solution)/shard_map/all_to_all | solution.py:212
  80.3 1.3 collective-permute-start.1
  81.6 0.8 collective-permute-start.2
  83.0 1.4 fusion.14
  84.5 69.1 %collective-permute-done.1 = bf16[256,256]{0,1:T(8,128)(2,1)S(1)} collective-permute-done((bf16[256,256]{0,1:T(8,128)(2,1)S(1)}, bf16[256,256]{0,1:T(8,128)(2,1)S(1)}, u32[]{:S(2)}, u32[]{:S(2)}) %collective-permute-start.1) | collective-permute-done | bytes 131104 | tf_op jit(solution)/shard_map/ppermute | solution.py:160
  153.8 11.7 %cholesky.44 = f32[128,128]{1,0:T(8,128)S(1)} custom-call(f32[128,128]{1,0:T(8,128)S(1)} %fusion.9), custom_call_target="Cholesky" | custom-call | tf_op jit(solution)/shard_map/jit(cholesky)/cholesky | solution.py:189
  166.9 9.8 %custom-call.6 = f32[1,128,128]{1,2,0:T(8,128)S(1)} custom-call(f32[1,128,128]{2,1,0:T(8,128)S(1)} %get-tuple-element.41), custom_call_target="InvertDiagBlocksLowerTriangular" | custom-call | tf_op jit(solution)/shard_map/jit(_solve_triangular)/triangular_solve | solution.py:170
  177.6 11.7 %cholesky.55 = f32[128,128]{1,0:T(8,128)S(1)} custom-call(f32[128,128]{1,0:T(8,128)S(1)} %fusion.7), custom_call_target="Cholesky" | custom-call | tf_op jit(solution)/shard_map/jit(cholesky)/cholesky | solution.py:193
  190.7 10.0 %custom-call.7 = f32[1,128,128]{1,2,0:T(8,128)S(1)} custom-call(f32[1,128,128]{2,1,0:T(8,128)S(1)} %get-tuple-element.39), custom_call_target="InvertDiagBlocksLowerTriangular" | custom-call | tf_op jit(solution)/shard_map/jit(_solve_triangular)/triangular_solve | solution.py:170
  201.0 6.4 %assemble.4 = (f32[40,32,256]{2,1,0:T(8,128)S(1)}, bf16[1280,256]{1,0:T(8,128)(2,1)S(1)}) custom-call(s32[512]{0:T(512)S(1)} %broadcast_select_fusion.target, s32[2]{0:T(128)S(1)} %pad_add_fusion.place, bf16[512,32,128]{2,1,0:T(8,128)(2,1)} %bitcast.3.x_ref, bf16[40,32,256]{2,1,0:T(8,128)(2,1)S(1)} %get-tuple-element.46.e_ref, f32[128,128]{1,0:T(8,128)S(1)} %bitcast.48, ...), custom_call_target="tpu_custom_call" | custom-call | flops 83886080 | bytes 4194304 | tf_op jit(solution)/shard_map/assemble/pallas_call | solution.py:85
  207.4 1.0 copy-done.2
  208.4 1.3 collective-permute-start.3
  209.7 5.6 %slice.108 = bf16[64,8,32,128]{3,2,1,0:T(8,128)(2,1)} slice(bf16[64,8,128,128]{3,2,1,0:T(8,128)(2,1)} %bitcast.57), slice={[0:64], [0:8], [80:112], [0:128]} | slice | bytes 8388608 | tf_op jit(solution)/shard_map/slice | solution.py:206
  215.3 14.4 %collective-permute-done.3.refs_4_ = bf16[1280,256]{1,0:T(8,128)(2,1)S(1)} collective-permute-done((bf16[1280,256]{1,0:T(8,128)(2,1)S(1)}, bf16[1280,256]{1,0:T(8,128)(2,1)S(1)}, u32[]{:S(2)}, u32[]{:S(2)}) %collective-permute-start.3) | collective-permute-done | bytes 655392 | tf_op jit(solution)/shard_map/ppermute | solution.py:220
  229.7 0.9 copy-done.8
  230.5 11.4 %all-to-all-start.2 = ((bf16[64,8,32,128]{3,2,1,0:T(8,128)(2,1)}), bf16[64,8,32,128]{3,2,1,0:T(8,128)(2,1)}, u32[]{:S(2)}, u32[]{:S(2)}) async-start(bf16[64,8,32,128]{3,2,1,0:T(8,128)(2,1)} %slice.108), calls=%async_computation.2 | async-start | bytes 8388608 | tf_op jit(solution)/shard_map/all_to_all | solution.py:212
  241.9 1.3 slice.131.e_ref
  243.2 7.5 %assemble.5 = (f32[40,48,256]{2,1,0:T(8,128)S(1)}, bf16[1920,256]{1,0:T(8,128)(2,1)S(1)}) custom-call(s32[512]{0:T(512)S(1)} %broadcast_select_fusion.target, s32[2]{0:T(128)S(1)} %pad_add_fusion.place, bf16[512,48,128]{2,1,0:T(8,128)(2,1)} %bitcast.14.x_ref, bf16[40,48,256]{2,1,0:T(8,128)(2,1)S(1)} %slice.131.e_ref, f32[128,128]{1,0:T(8,128)S(1)} %bitcast.49, ...), custom_call_target="tpu_custom_call" | custom-call | flops 125829120 | bytes 6291456 | tf_op jit(solution)/shard_map/assemble/pallas_call | solution.py:85
  250.7 1.3 copy-done
  252.0 1.3 collective-permute-start.4
  253.3 3.7 slice.112
  256.9 39.9 %all-to-all-done.2 = bf16[64,8,32,128]{3,2,1,0:T(8,128)(2,1)} async-done(((bf16[64,8,32,128]{3,2,1,0:T(8,128)(2,1)}), bf16[64,8,32,128]{3,2,1,0:T(8,128)(2,1)}, u32[]{:S(2)}, u32[]{:S(2)}) %all-to-all-start.2) | async-done | bytes 4194336 | tf_op jit(solution)/shard_map/all_to_all | solution.py:212
  296.8 12.8 %collective-permute-done.4.refs_5_ = bf16[1920,256]{1,0:T(8,128)(2,1)S(1)} collective-permute-done((bf16[1920,256]{1,0:T(8,128)(2,1)S(1)}, bf16[1920,256]{1,0:T(8,128)(2,1)S(1)}, u32[]{:S(2)}, u32[]{:S(2)}) %collective-permute-start.4) | collective-permute-done | bytes 983072 | tf_op jit(solution)/shard_map/ppermute | solution.py:220
  309.7 0.9 copy-done.6
  310.6 10.2 %all-to-all-start.3 = ((bf16[64,8,16,128]{3,2,1,0:T(8,128)(2,1)}), bf16[64,8,16,128]{3,2,1,0:T(8,128)(2,1)S(1)}, u32[]{:S(2)}, u32[]{:S(2)}) async-start(bf16[64,8,16,128]{3,2,1,0:T(8,128)(2,1)} %slice.112), calls=%async_computation.3 | async-start | bytes 4194304 | tf_op jit(solution)/shard_map/all_to_all | solution.py:212
  320.9 7.5 %assemble.6 = (f32[40,32,256]{2,1,0:T(8,128)S(1)}, bf16[1280,256]{1,0:T(8,128)(2,1)}) custom-call(s32[512]{0:T(512)S(1)} %broadcast_select_fusion.target, s32[2]{0:T(128)S(1)} %pad_add_fusion.place, bf16[512,32,128]{2,1,0:T(8,128)(2,1)} %bitcast.15.x_ref, bf16[40,32,256]{2,1,0:T(8,128)(2,1)S(1)} %get-tuple-element.45.e_ref, f32[128,128]{1,0:T(8,128)S(1)} %bitcast.50, ...), custom_call_target="tpu_custom_call" | custom-call | flops 83886080 | bytes 4194304 | tf_op jit(solution)/shard_map/assemble/pallas_call | solution.py:85
  328.3 1.1 copy-done.4
  329.4 1.3 collective-permute-start.5
  330.7 0.8 slice.119
  331.4 0.8 slice.120
  333.7 1.3 collective-permute-start.8
  335.0 1.3 collective-permute-start.9
  336.3 10.8 %all-to-all-done.3 = bf16[64,8,16,128]{3,2,1,0:T(8,128)(2,1)S(1)} async-done(((bf16[64,8,16,128]{3,2,1,0:T(8,128)(2,1)}), bf16[64,8,16,128]{3,2,1,0:T(8,128)(2,1)S(1)}, u32[]{:S(2)}, u32[]{:S(2)}) %all-to-all-start.3) | async-done | bytes 2097184 | tf_op jit(solution)/shard_map/all_to_all | solution.py:212
  347.1 2.0 assemble.7
  349.1 1.3 collective-permute-start.6
  350.4 8.0 %collective-permute-done.5.refs_6_ = bf16[1280,256]{1,0:T(8,128)(2,1)} collective-permute-done((bf16[1280,256]{1,0:T(8,128)(2,1)}, bf16[1280,256]{1,0:T(8,128)(2,1)}, u32[]{:S(2)}, u32[]{:S(2)}) %collective-permute-start.5) | collective-permute-done | bytes 655392 | tf_op jit(solution)/shard_map/ppermute | solution.py:220
  359.2 1.0 fusion.2
  360.8 1.3 collective-permute-start.11
  362.8 2.0 collective-permute-done.6.refs_7_
  364.9 5.4 %collective-permute-done.11 = bf16[2,16,256]{2,1,0:T(8,128)(2,1)S(1)} collective-permute-done((bf16[2,16,256]{2,1,0:T(8,128)(2,1)S(1)}, bf16[2,16,256]{2,1,0:T(8,128)(2,1)S(1)}, u32[]{:S(2)}, u32[]{:S(2)}) %collective-permute-start.11) | collective-permute-done | bytes 16416 | tf_op jit(solution)/shard_map/ppermute | solution.py:160
  370.3 1.3 copy-done.5
  371.6 1.2 copy-done.7
  372.8 1.1 copy-done.9
  373.9 7.4 %update.1 = f32[40,128,256]{2,1,0:T(8,128)} custom-call(s32[2]{0:T(128)S(1)} %pad_add_fusion.place, f32[40,32,256]{2,1,0:T(8,128)S(1)} %copy-done.3, f32[40,48,256]{2,1,0:T(8,128)S(1)} %copy-done.1, f32[40,32,256]{2,1,0:T(8,128)S(1)} %copy-done.5, f32[40,16,256]{2,1,0:T(8,128)S(1)} %get-tuple-element.36.refs_3_, bf16[1280,256]{1,0:T(8,128)(2,1)S(1)} %copy-done.9, ...), custom_call_target="tpu_custom_call" | custom-call | tf_op jit(solution)/shard_map/update/pallas_call | solution.py:139
  (82 shorter events, 9.0 us)
Async XLA Ops:
  5.6 65.0 %all-to-all-start = ((bf16[64,8,32,128]{3,2,1,0:T(8,128)(2,1)}), bf16[64,8,32,128]{3,2,1,0:T(8,128)(2,1)}, u32[]{:S(2)}, u32[]{:S(2)}) async-start(bf16[64,8,32,128]{3,2,1,0:T(8,128)(2,1)} %slice.124), calls=%async_computation | async-start | bytes 8388608 | tf_op jit(solution)/shard_map/all_to_all | solution.py:212
  70.5 9.0 %slice-start.2 = ((bf16[1,5120,256]{2,1,0:T(8,128)(2,1)}), bf16[1,256,256]{2,1,0:T(8,128)(2,1)S(1)}, s32[]{:S(2)}) async-start(bf16[1,5120,256]{2,1,0:T(8,128)(2,1)} %param.8), calls=%async_computation.6 | async-start | bytes 262144 | tf_op jit(solution)/shard_map/slice | solution.py:185
  70.5 11.9 %copy-start.13 = (s32[1,1,1,16,4,8]{3,5,4,2,1,0:T(8,128)S(1)}, s32[1,1,1,16,4,8]{3,5,4,2,1,0:T(8,128)}, u32[]{:S(2)}) copy-start(s32[1,1,1,16,4,8]{3,5,4,2,1,0:T(8,128)} %param.11) | copy-start | bytes 6148
  70.5 11.9 %copy-start.14 = (s32[1,1,1,16,4,8]{3,5,4,2,1,0:T(8,128)S(1)}, s32[1,1,1,16,4,8]{3,5,4,2,1,0:T(8,128)}, u32[]{:S(2)}) copy-start(s32[1,1,1,16,4,8]{3,5,4,2,1,0:T(8,128)} %param.12) | copy-start | bytes 6148
  70.6 12.1 %copy-start.15 = (s32[1,1,1,16,4]{3,4,2,1,0:T(4,128)S(1)}, s32[1,1,1,16,4]{3,4,2,1,0:T(4,128)}, u32[]{:S(2)}) copy-start(s32[1,1,1,16,4]{3,4,2,1,0:T(4,128)} %param.10) | copy-start | bytes 772
  70.6 144.7 %all-to-all-start.1 = ((bf16[64,8,48,128]{3,2,1,0:T(8,128)(2,1)}), bf16[64,8,48,128]{3,2,1,0:T(8,128)(2,1)}, u32[]{:S(2)}, u32[]{:S(2)}) async-start(bf16[64,8,48,128]{3,2,1,0:T(8,128)(2,1)} %slice.104), calls=%async_computation.1 | async-start | bytes 12582912 | tf_op jit(solution)/shard_map/all_to_all | solution.py:212
  79.6 4.9 %collective-permute-start = (bf16[256,256]{0,1:T(8,128)(2,1)S(1)}, bf16[256,256]{0,1:T(8,128)(2,1)S(1)}, u32[]{:S(2)}, u32[]{:S(2)}) collective-permute-start(bf16[256,256]{0,1:T(8,128)(2,1)S(1)} %bitcast.62), channel_id=1, source_target_pairs={{0,2},{1,3},{8,10},{9,11},{16,18},{17,19},{24,26},{25,27},{32,34},... | collective-permute-start | bytes 393224 | tf_op jit(solution)/shard_map/ppermute | solution.py:160
  80.3 73.4 %collective-permute-start.1 = (bf16[256,256]{0,1:T(8,128)(2,1)S(1)}, bf16[256,256]{0,1:T(8,128)(2,1)S(1)}, u32[]{:S(2)}, u32[]{:S(2)}) collective-permute-start(bf16[256,256]{0,1:T(8,128)(2,1)S(1)} %bitcast.63), channel_id=1, source_target_pairs={{0,4},{1,5},{8,12},{9,13},{16,20},{17,21},{24,28},{25,29},{32,36},... | collective-permute-start | bytes 393224 | tf_op jit(solution)/shard_map/ppermute | solution.py:160
  81.6 72.1 %collective-permute-start.2 = (bf16[256,256]{0,1:T(8,128)(2,1)S(1)}, bf16[256,256]{0,1:T(8,128)(2,1)S(1)}, u32[]{:S(2)}, u32[]{:S(2)}) collective-permute-start(bf16[256,256]{0,1:T(8,128)(2,1)S(1)} %bitcast.64), channel_id=1, source_target_pairs={{0,6},{1,7},{8,14},{9,15},{16,22},{17,23},{24,30},{25,31},{32,38},... | collective-permute-start | bytes 393224 | tf_op jit(solution)/shard_map/ppermute | solution.py:160
  207.4 1.1 copy-start.2
  208.4 6.9 %copy-start.11 = (bf16[1280,256]{1,0:T(8,128)(2,1)}, bf16[1280,256]{1,0:T(8,128)(2,1)S(1)}, u32[]{:S(2)}) copy-start(bf16[1280,256]{1,0:T(8,128)(2,1)S(1)} %get-tuple-element.29) | copy-start | bytes 1966084
  208.4 21.3 %collective-permute-start.3 = (bf16[1280,256]{1,0:T(8,128)(2,1)S(1)}, bf16[1280,256]{1,0:T(8,128)(2,1)S(1)}, u32[]{:S(2)}, u32[]{:S(2)}) collective-permute-start(bf16[1280,256]{1,0:T(8,128)(2,1)S(1)} %get-tuple-element.29), channel_id=1, source_target_pairs={{0,1},{2,3},{4,5},{6,7},{8,9},{10,11},{12,13},{14,15},{16,17},{18,... | collective-permute-start | bytes 1966088 | tf_op jit(solution)/shard_map/ppermute | solution.py:220
  229.7 0.9 copy-start.8
  230.5 66.3 %all-to-all-start.2 = ((bf16[64,8,32,128]{3,2,1,0:T(8,128)(2,1)}), bf16[64,8,32,128]{3,2,1,0:T(8,128)(2,1)}, u32[]{:S(2)}, u32[]{:S(2)}) async-start(bf16[64,8,32,128]{3,2,1,0:T(8,128)(2,1)} %slice.108), calls=%async_computation.2 | async-start | bytes 8388608 | tf_op jit(solution)/shard_map/all_to_all | solution.py:212
  250.7 1.3 copy-start
  252.0 57.7 %copy-start.10 = (bf16[1920,256]{1,0:T(8,128)(2,1)}, bf16[1920,256]{1,0:T(8,128)(2,1)S(1)}, u32[]{:S(2)}) copy-start(bf16[1920,256]{1,0:T(8,128)(2,1)S(1)} %get-tuple-element.34) | copy-start | bytes 2949124
  252.0 57.7 %collective-permute-start.4 = (bf16[1920,256]{1,0:T(8,128)(2,1)S(1)}, bf16[1920,256]{1,0:T(8,128)(2,1)S(1)}, u32[]{:S(2)}, u32[]{:S(2)}) collective-permute-start(bf16[1920,256]{1,0:T(8,128)(2,1)S(1)} %get-tuple-element.34), channel_id=1, source_target_pairs={{0,1},{2,3},{4,5},{6,7},{8,9},{10,11},{12,13},{14,15},{16,17},{18,... | collective-permute-start | bytes 2949128 | tf_op jit(solution)/shard_map/ppermute | solution.py:220
  309.7 0.9 copy-start.6
  310.6 36.5 %all-to-all-start.3 = ((bf16[64,8,16,128]{3,2,1,0:T(8,128)(2,1)}), bf16[64,8,16,128]{3,2,1,0:T(8,128)(2,1)S(1)}, u32[]{:S(2)}, u32[]{:S(2)}) async-start(bf16[64,8,16,128]{3,2,1,0:T(8,128)(2,1)} %slice.112), calls=%async_computation.3 | async-start | bytes 4194304 | tf_op jit(solution)/shard_map/all_to_all | solution.py:212
  320.8 15.5 %copy-start.12 = (bf16[1,5120,256]{2,1,0:T(8,128)(2,1)S(1)}, bf16[1,5120,256]{2,1,0:T(8,128)(2,1)}, u32[]{:S(2)}) copy-start(bf16[1,5120,256]{2,1,0:T(8,128)(2,1)} %param.8) | copy-start | bytes 7864324
  320.8 38.3 %slice-start = ((bf16[1920,256]{1,0:T(8,128)(2,1)}), bf16[96,256]{1,0:T(8,128)(2,1)S(1)}, s32[]{:S(2)}) async-start(bf16[1920,256]{1,0:T(8,128)(2,1)} %copy-done.6), calls=%async_computation.4 | async-start | bytes 98304 | tf_op jit(solution)/shard_map/slice | solution.py:226
  320.8 38.3 %slice-start.1 = ((bf16[1280,256]{1,0:T(8,128)(2,1)}), bf16[64,256]{1,0:T(8,128)(2,1)S(1)}, s32[]{:S(2)}) async-start(bf16[1280,256]{1,0:T(8,128)(2,1)} %copy-done.8), calls=%async_computation.5 | async-start | bytes 65536 | tf_op jit(solution)/shard_map/slice | solution.py:226
  328.3 1.1 copy-start.4
  329.4 29.0 %collective-permute-start.5 = (bf16[1280,256]{1,0:T(8,128)(2,1)}, bf16[1280,256]{1,0:T(8,128)(2,1)}, u32[]{:S(2)}, u32[]{:S(2)}) collective-permute-start(bf16[1280,256]{1,0:T(8,128)(2,1)} %get-tuple-element.37), channel_id=1, source_target_pairs={{0,1},{2,3},{4,5},{6,7},{8,9},{10,11},{12,13},{14,15},{16,17},{18,... | collective-permute-start | bytes 1966088 | tf_op jit(solution)/shard_map/ppermute | solution.py:220
  333.0 26.2 %collective-permute-start.7 = (bf16[2,112,256]{2,1,0:T(8,128)(2,1)S(1)}, bf16[2,112,256]{2,1,0:T(8,128)(2,1)S(1)}, u32[]{:S(2)}, u32[]{:S(2)}) collective-permute-start(bf16[2,112,256]{2,1,0:T(8,128)(2,1)S(1)} %pad_maximum_fusion.1), channel_id=1, source_target_pairs={{0,3},{8,11},{16,19},{24,27},{32,35},{40,43},{48,51},{56,59},{64,6... | collective-permute-start | bytes 344072 | tf_op jit(solution)/shard_map/ppermute | solution.py:160
  333.7 25.5 %collective-permute-start.8 = (bf16[2,112,256]{2,1,0:T(8,128)(2,1)S(1)}, bf16[2,112,256]{2,1,0:T(8,128)(2,1)S(1)}, u32[]{:S(2)}, u32[]{:S(2)}) collective-permute-start(bf16[2,112,256]{2,1,0:T(8,128)(2,1)S(1)} %pad_maximum_fusion.1), channel_id=1, source_target_pairs={{0,5},{8,13},{16,21},{24,29},{32,37},{40,45},{48,53},{56,61},{64,6... | collective-permute-start | bytes 344072 | tf_op jit(solution)/shard_map/ppermute | solution.py:160
  335.0 24.2 %collective-permute-start.9 = (bf16[2,112,256]{2,1,0:T(8,128)(2,1)S(1)}, bf16[2,112,256]{2,1,0:T(8,128)(2,1)}, u32[]{:S(2)}, u32[]{:S(2)}) collective-permute-start(bf16[2,112,256]{2,1,0:T(8,128)(2,1)S(1)} %pad_maximum_fusion.1), channel_id=1, source_target_pairs={{0,7},{8,15},{16,23},{24,31},{32,39},{40,47},{48,55},{56,63},{64,7... | collective-permute-start | bytes 344072 | tf_op jit(solution)/shard_map/ppermute | solution.py:160
  347.1 23.2 %copy-start.1 = (f32[40,48,256]{2,1,0:T(8,128)S(1)}, f32[40,48,256]{2,1,0:T(8,128)}, u32[]{:S(2)}) copy-start(f32[40,48,256]{2,1,0:T(8,128)} %copy-done) | copy-start | bytes 5898244
  347.1 23.2 %copy-start.3 = (f32[40,32,256]{2,1,0:T(8,128)S(1)}, f32[40,32,256]{2,1,0:T(8,128)}, u32[]{:S(2)}) copy-start(f32[40,32,256]{2,1,0:T(8,128)} %copy-done.2) | copy-start | bytes 3932164
  349.1 15.7 %collective-permute-start.6 = (bf16[640,256]{1,0:T(8,128)(2,1)S(1)}, bf16[640,256]{1,0:T(8,128)(2,1)S(1)}, u32[]{:S(2)}, u32[]{:S(2)}) collective-permute-start(bf16[640,256]{1,0:T(8,128)(2,1)S(1)} %get-tuple-element.38), channel_id=1, source_target_pairs={{0,1},{2,3},{4,5},{6,7},{8,9},{10,11},{12,13},{14,15},{16,17},{18,... | collective-permute-start | bytes 983048 | tf_op jit(solution)/shard_map/ppermute | solution.py:220
  360.2 4.7 %collective-permute-start.10 = (bf16[2,16,256]{2,1,0:T(8,128)(2,1)S(1)}, bf16[2,16,256]{2,1,0:T(8,128)(2,1)S(1)}, u32[]{:S(2)}, u32[]{:S(2)}) collective-permute-start(bf16[2,16,256]{2,1,0:T(8,128)(2,1)S(1)} %bitcast.70), channel_id=1, source_target_pairs={{0,3},{8,11},{16,19},{24,27},{32,35},{40,43},{48,51},{56,59},{64,6... | collective-permute-start | bytes 49160 | tf_op jit(solution)/shard_map/ppermute | solution.py:160
  360.8 9.4 %collective-permute-start.11 = (bf16[2,16,256]{2,1,0:T(8,128)(2,1)S(1)}, bf16[2,16,256]{2,1,0:T(8,128)(2,1)S(1)}, u32[]{:S(2)}, u32[]{:S(2)}) collective-permute-start(bf16[2,16,256]{2,1,0:T(8,128)(2,1)S(1)} %bitcast.71), channel_id=1, source_target_pairs={{0,5},{8,13},{16,21},{24,29},{32,37},{40,45},{48,53},{56,61},{64,6... | collective-permute-start | bytes 49160 | tf_op jit(solution)/shard_map/ppermute | solution.py:160
  362.1 8.1 %collective-permute-start.12 = (bf16[2,16,256]{2,1,0:T(8,128)(2,1)S(1)}, bf16[2,16,256]{2,1,0:T(8,128)(2,1)S(1)}, u32[]{:S(2)}, u32[]{:S(2)}) collective-permute-start(bf16[2,16,256]{2,1,0:T(8,128)(2,1)S(1)} %bitcast.72), channel_id=1, source_target_pairs={{0,7},{8,15},{16,23},{24,31},{32,39},{40,47},{48,55},{56,63},{64,7... | collective-permute-start | bytes 49160 | tf_op jit(solution)/shard_map/ppermute | solution.py:160
  370.3 1.3 copy-start.5
  371.6 1.2 copy-start.7
  372.8 1.1 copy-start.9

commit v2 on v0

v2 whole, which is shorter than its diff:
```python
import functools

import jax
import jax.numpy as jnp
from jax import lax
from jax.experimental import pallas as pl
from jax.experimental.pallas import tpu as pltpu
from jax.sharding import PartitionSpec as P

PB = 128
CHUNKS = (48, 80)
PIECES = ((0, 0, 16), (0, 16, 32), (1, 0, 48), (1, 48, 32))
CHAINS = 4
DEPTH = 4
BLOCK = 64
EXACT = lax.Precision.HIGHEST
VMEM = pl.BlockSpec(memory_space=pltpu.VMEM)


def dot_t(a, b):
    return lax.dot_general(a, b, (((1,), (1,)), ((), ())), preferred_element_type=jnp.float32)


def assemble_kernel(
    rows, offset, start, target, place, x_hbm, e_hbm, t1_ref, t2_ref, l21_ref, l11_ref, l22_ref, *refs
):
    f_hbm, h_hbm, x_ref, e_ref, f_ref, h_ref, x_sem, e_sem, f_sem, h_sem = refs[-CHAINS - 10 : -CHAINS]
    acc = refs[-CHAINS:]
    slots, tiles = x_ref.shape[0], e_ref.shape[0]
    here = slice(start, start + rows)

    def bring(b):
        part = pl.ds(b * BLOCK, BLOCK)
        return pltpu.make_async_copy(
            x_hbm.at[part, pl.ds(offset, rows), :], x_ref.at[part], x_sem.at[b]
        )

    for b in range(slots // BLOCK):
        bring(b).start()
    entries = pltpu.make_async_copy(e_hbm.at[:, pl.ds(start, rows), :], e_ref, e_sem)
    entries.start()
    for a in acc:
        a[...] = jnp.zeros_like(a)
    group = CHAINS * DEPTH
    for b in range(slots // BLOCK):
        bring(b).wait()

        def add(i, carry):
            base = b * BLOCK + i * group
            spot = [pl.multiple_of(target[base + k] * rows, rows) for k in range(group)]
            for d in range(DEPTH):
                values = []
                for k, a in enumerate(acc):
                    where = pl.ds(spot[d * CHAINS + k], rows)
                    tile = x_ref[base + d * CHAINS + k].astype(jnp.float32)
                    values.append((where, a[where, :] + tile))
                for a, (where, value) in zip(acc, values):
                    a[where, :] = value
            return carry

        lax.fori_loop(0, BLOCK // group, add, 0)
    entries.wait()

    batch = 8
    span = batch * rows
    copies = []
    for g in range(tiles // batch):
        out = slice(g * batch, (g + 1) * batch)
        flat = slice(g * span, (g + 1) * span)
        parts = []
        for c in range(2):
            lines = slice((c * tiles + g * batch) * rows, (c * tiles + g * batch) * rows + span)
            total = e_ref[out, :, c * PB : (c + 1) * PB].astype(jnp.float32).reshape(span, PB)
            for a in acc:
                total += a[lines, :]
            parts.append(total)
        left, right = parts

        @pl.when(place[1] == 1)
        def _():
            f_ref[out, :, :PB] = left.reshape(batch, rows, PB)
            f_ref[out, :, PB:] = right.reshape(batch, rows, PB)

        @pl.when(place[1] == 0)
        def _():
            x1 = jnp.dot(left, t1_ref[...], precision=EXACT, preferred_element_type=jnp.float32)
            if g == 0:
                top = jnp.concatenate([l11_ref[here, :], x1[rows:]], axis=0)
                x1 = jnp.where(place[0] == 0, top, x1)
            h1 = x1.astype(jnp.bfloat16)
            right2 = right - dot_t(h1, l21_ref[...])
            x2 = jnp.dot(right2, t2_ref[...], precision=EXACT, preferred_element_type=jnp.float32)
            if g == 0:
                top = [jnp.zeros((rows, PB), jnp.float32), l22_ref[here, :], x2[2 * rows :]]
                x2 = jnp.where(place[0] == 0, jnp.concatenate(top, axis=0), x2)
            h_ref[flat, :PB] = h1
            h_ref[flat, PB:] = x2.astype(jnp.bfloat16)
            f_ref[out, :, :PB] = x1.reshape(batch, rows, PB)
            f_ref[out, :, PB:] = x2.reshape(batch, rows, PB)

        copies.append(pltpu.make_async_copy(h_ref.at[flat], h_hbm.at[flat], h_sem.at[g]))
        copies.append(pltpu.make_async_copy(f_ref.at[out], f_hbm.at[out, pl.ds(start, rows), :], f_sem.at[g]))
        for copy in copies[-2:]:
            copy.start()
    for copy in copies:
        copy.wait()


def assemble(target, place, received, offset, entries, start, rows, t1, t2, l21, l11, l22, base):
    slots = received.shape[0]
    tiles = entries.shape[0]
    anywhere = pl.BlockSpec(memory_space=pl.ANY)
    square = pl.BlockSpec((PB, PB), lambda i, *_: (0, 0))
    extra = [] if base is None else [base]
    front = jax.ShapeDtypeStruct((tiles, PB, 2 * PB), jnp.float32)
    half = jax.ShapeDtypeStruct((tiles * rows, 2 * PB), jnp.bfloat16)
    return pl.pallas_call(
        functools.partial(assemble_kernel, rows, offset, start),
        grid_spec=pltpu.PrefetchScalarGridSpec(
            num_scalar_prefetch=2,
            grid=(1,),
            in_specs=[anywhere, anywhere] + [square] * 5 + [anywhere] * len(extra),
            out_specs=[anywhere, anywhere],
            scratch_shapes=[
                pltpu.VMEM((slots, rows, PB), jnp.bfloat16),
                pltpu.VMEM((tiles, rows, 2 * PB), jnp.bfloat16),
                pltpu.VMEM((tiles, rows, 2 * PB), front.dtype),
                pltpu.VMEM(half.shape, half.dtype),
                pltpu.SemaphoreType.DMA((slots // BLOCK,)),
                pltpu.SemaphoreType.DMA,
                pltpu.SemaphoreType.DMA((tiles // 8,)),
                pltpu.SemaphoreType.DMA((tiles // 8,)),
            ]
            + [pltpu.VMEM(((2 * tiles + 1) * rows, PB), jnp.float32)] * CHAINS,
        ),
        out_shape=[front, half],
        input_output_aliases={9: 0} if extra else {},
        compiler_params=pltpu.CompilerParams(
            dimension_semantics=("arbitrary",), vmem_limit_bytes=48 * 1024 * 1024
        ),
        cost_estimate=pl.CostEstimate(
            flops=slots * rows * PB * 40, bytes_accessed=slots * rows * PB * 2, transcendentals=0
        ),
        name="assemble",
    )(target, place, received, entries, t1, t2, l21, l11, l22, *extra)


def update_kernel(pieces, place, p_hbm, *refs):
    n = len(pieces)
    halves = refs[:n]
    out_hbm, p_ref, f_ref, h_ref, p_sem, f_sem, h_sem, o_sem = refs[n + 1 :]
    tiles, first = f_ref.shape[0], pieces[0][0]
    batch = 8

    @pl.when(place[1] == 1)
    def _():
        columns = pltpu.make_async_copy(p_hbm, p_ref, p_sem)
        columns.start()
        steps = []
        for g in range(tiles // batch):
            out = slice(g * batch, (g + 1) * batch)
            for h_hbm, (start, rows) in zip(halves, pieces):
                k = len(steps)
                at = pl.ds(start, rows)
                local = pl.ds(start - first, rows)
                lines = pl.ds((start - first) * tiles + g * batch * rows, batch * rows)
                near = f_ref.at[out, local, :]
                bring = [
                    pltpu.make_async_copy(out_hbm.at[out, at, :], near, f_sem.at[k]),
                    pltpu.make_async_copy(
                        h_hbm.at[pl.ds(g * batch * rows, batch * rows)], h_ref.at[lines], h_sem.at[k]
                    ),
                ]
                give = pltpu.make_async_copy(near, out_hbm.at[out, at, :], o_sem.at[k])
                for copy in bring:
                    copy.start()
                steps.append((out, local, lines, rows, bring, give))
        columns.wait()
        for out, local, lines, rows, bring, give in steps:
            for copy in bring:
                copy.wait()
            change = dot_t(h_ref[lines, :], p_ref[...])
            f_ref[out, local, :] -= change.reshape(batch, rows, 2 * PB)
            give.start()
        for step in steps:
            step[-1].wait()


def update(place, front, halves, pieces, columns):
    tiles = front.shape[0]
    rows = sum(r for _, r in pieces)
    steps = len(pieces) * (tiles // 8)
    anywhere = pl.BlockSpec(memory_space=pl.ANY)
    return pl.pallas_call(
        functools.partial(update_kernel, pieces),
        grid_spec=pltpu.PrefetchScalarGridSpec(
            num_scalar_prefetch=1,
            grid=(1,),
            in_specs=[anywhere] * (2 + len(pieces)),
            out_specs=anywhere,
            scratch_shapes=[
                pltpu.VMEM(columns.shape, columns.dtype),
                pltpu.VMEM((tiles, rows, 2 * PB), jnp.float32),
                pltpu.VMEM((tiles * rows, 2 * PB), jnp.bfloat16),
                pltpu.SemaphoreType.DMA,
                pltpu.SemaphoreType.DMA((steps,)),
                pltpu.SemaphoreType.DMA((steps,)),
                pltpu.SemaphoreType.DMA((steps,)),
            ],
        ),
        out_shape=jax.ShapeDtypeStruct(front.shape, front.dtype),
        input_output_aliases={2 + len(pieces): 0},
        compiler_params=pltpu.CompilerParams(
            dimension_semantics=("arbitrary",), vmem_limit_bytes=48 * 1024 * 1024
        ),
        cost_estimate=pl.CostEstimate(
            flops=2 * tiles * rows * 4 * PB * PB, bytes_accessed=tiles * rows * PB * 20, transcendentals=0
        ),
        name="update",
    )(place, columns, *halves, front)


def from_first(x, axes, targets, own):
    total = own
    for t in targets:
        total = total + lax.ppermute(x, axes, [(0, t)])
    return total


def after(x, other):
    return lax.optimization_barrier((x, other))[0]


def exchange(x):
    return lax.all_to_all(x, ("group", "row"), split_axis=0, concat_axis=0, tiled=True)


def inverse_t(factor):
    eye = jnp.eye(PB, dtype=jnp.float32)
    return jax.scipy.linalg.solve_triangular(factor, eye, lower=True).T


def local(front_entries, contrib, counts, tile_rows, tile_cols):
    entries = front_entries[0]
    row, col = lax.axis_index("row"), lax.axis_index("col")
    place = jnp.stack([row, col]).astype(jnp.int32)
    tiles = entries.shape[0] // PB
    owners = contrib.shape[3] * contrib.shape[4]
    slots = contrib.shape[5]
    outgoing = contrib.reshape(owners, slots, PB, PB)
    live = jnp.arange(slots, dtype=jnp.int32)[None, :] < counts.reshape(owners)[:, None]
    target = tile_cols.reshape(owners, slots) * tiles + tile_rows.reshape(owners, slots)
    target = jnp.where(live, target, 2 * tiles).reshape(owners * slots)

    lead = entries[: 2 * PB]
    lead = from_first(
        lead, "row", (1, 2, 3), jnp.where(row == 0, lead, jnp.zeros_like(lead))
    ).astype(jnp.float32)
    l11 = jnp.linalg.cholesky(lead[:PB, :PB])
    t1 = inverse_t(l11)
    l21 = jnp.dot(lead[PB:, :PB], t1, precision=EXACT).astype(jnp.bfloat16)
    rest = lead[PB:, PB:] - dot_t(l21, l21)
    l22 = jnp.linalg.cholesky(rest)
    t2 = inverse_t(l22)

    shaped = entries.reshape(tiles, PB, 2 * PB)
    ready = (target, place, t1, t2, l11, l21, l22)
    piece = after(outgoing[:, :, : CHUNKS[0]], lead)
    first = exchange(piece)
    piece = after(outgoing, piece)[:, :, CHUNKS[0] :]
    first, second = lax.optimization_barrier((first, exchange(after(piece, (first, ready)))))
    received = [r.reshape(owners * slots, -1, PB) for r in (first, second)]

    halves, columns, rows_of = [], [], []
    front, start = None, 0
    for chunk, offset, rows in PIECES:
        tiles_in = received[chunk]
        if len(halves) >= 2:
            tiles_in = after(tiles_in, halves[-2])
        front, h = assemble(
            target, place, tiles_in, offset, shaped, start, rows, t1, t2, l21, l11, l22, front
        )
        columns.append(h[2 * rows : 4 * rows].reshape(2, rows, 2 * PB))
        rows_of.append((start, rows))
        start += rows
        if start == PB:
            columns = jnp.concatenate(columns, axis=1).reshape(2 * PB, 2 * PB)
            columns = from_first(columns, ("row", "col"), (1, 3, 5, 7), jnp.zeros_like(columns))
            h = after(h, columns)
        if len(halves) == 1:
            h = after(h, halves[0])
        halves.append(lax.ppermute(h, "col", [(0, 1)]))
    front = update(place, front, halves[:-1], rows_of[:-1], columns)
    front = update(place, front, halves[-1:], rows_of[-1:], columns)
    return front.reshape(front_entries.shape)


def solution(mesh):
    placed = (
        P("group", "row", "col"),
        P("group", "row", "col", None, None, None, None, None),
        P("group", "row", "col", None, None),
        P("group", "row", "col", None, None, None),
        P("group", "row", "col", None, None, None),
    )
    return jax.shard_map(
        local, mesh=mesh, in_specs=placed, out_specs=P("group", "row", "col"), check_vma=False
    )
```

time: 687 us -> 320 us (0.47)
  waiting for transfers between devices: 502 us -> 65.9 us
  blocking collectives: 0 us -> 128 us
  local copies, waits for them, and re-layouts: 65 us -> 20.5 us
  Pallas kernels: 0 us -> 32.5 us
  matrix products: 26.9 us -> 0.92 us
  other arithmetic: 65 us -> 46.2 us
  between operations: 13.8 us -> 0.6 us
  starting transfers between devices: 10.8 us -> 23.9 us
    psum x6 -> x0, waiting for transfers between devices: 267 us -> none  [spread(): return lax.psum(jnp.where(mine, x, jnp.zeros_like(x)), axis)]
    all_to_all x1, waiting for transfers between devices: 235 us -> 23.3 us  [exchange(): lax.all_to_all(x, ('group', 'row'), split_axis=0, concat_axis=0, tiled=True)]
    all_to_all x0 -> x1, blocking collectives: none -> 128 us  [exchange(): lax.all_to_all(x, ('group', 'row'), split_axis=0, concat_axis=0, tiled=True)]
    ppermute x0 -> x11, waiting for transfers between devices: none -> 42.6 us  [the longest x4 27.8 us: local(): halves.append(lax.ppermute(h, 'col', [(0, 1)]))]
    pallas_call x0 -> x6, Pallas kernels: none -> 32.5 us  [the longest x4 20.5 us: assemble(): pl.pallas_call(functools.partial(assemble_kernel, rows, offset, start), g...]
    unnamed x16 -> x10, local copies, waits for them, and re-layouts: 29.6 us -> 0.21 us
    dot_general x1 -> x0, local copies, waits for them, and re-layouts: 22.5 us -> none  [local(): assembled = jnp.dot(onehot, received, preferred_element_type=jnp.float32)]
    slice x4 -> x9, local copies, waits for them, and re-layouts: 0.19 us -> 19.7 us  [the longest x1 11.3 us: local(): piece = after(outgoing, piece)[:, :, CHUNKS[0]:]]
  transfers between devices with their start and end apart: 7 -> 12, of which waited for: 7 -> 5; matrix products, arithmetic and copies ran while one was open for 1% -> 21% of each run, Pallas kernels for 0% -> 8%
where the time goes in v2:
time: 320 us; the launch traced here: 319 us
  blocking collectives  128 us (40%)
  waiting for transfers between devices  65.9 us (21%)
  other arithmetic  46.2 us (14%)
  Pallas kernels  32.5 us (10%)
  starting transfers between devices  23.9 us (7%)
  local copies, waits for them, and re-layouts  20.5 us (6%)
    all_to_all x1, blocking collectives, exchange(): lax.all_to_all(x, ('group', 'row'), split_axis=0, concat_axis=0, tiled=True)  128 us
    ppermute x4, waiting for transfers between devices, local(): halves.append(lax.ppermute(h, 'col', [(0, 1)]))  27.8 us
    all_to_all x1, waiting for transfers between devices, exchange(): lax.all_to_all(x, ('group', 'row'), split_axis=0, concat_axis=0, tiled=True)  23.3 us
    another operation x4, other arithmetic, inverse_t(): return jax.scipy.linalg.solve_triangular(factor, eye, lower=True).T  21.1 us
    pallas_call x4, Pallas kernels, assemble(): pl.pallas_call(functools.partial(assemble_kernel, rows, offset, start), g...  20.5 us
    ppermute x7, waiting for transfers between devices, from_first(): total = total + lax.ppermute(x, axes, [(0, t)])  14.7 us
    all_to_all x1, starting transfers between devices, exchange(): lax.all_to_all(x, ('group', 'row'), split_axis=0, concat_axis=0, tiled=True)  12.8 us
    another operation x3, other arithmetic, local(): l11 = jnp.linalg.cholesky(lead[:PB, :PB])  12.4 us
  transfers between devices with their start and end apart: 12, of which 5 were waited for; matrix products, arithmetic and copies ran while one was open for 21% of the time, Pallas kernels for 8%

profile of v2, /device:TPU:14, one launch (start us, length us, event | category | flops | bytes accessed | tf_op | source)
XLA Modules:
  0.0 318.5 jit_solution(4008456253906469709)
XLA Ops:
  0.0 0.9 slice.42
  0.9 0.1 copy.28
  1.0 1.3 collective-permute-start.1
  2.3 0.7 collective-permute-start
  3.0 0.7 collective-permute-start.2
  3.7 7.4 %slice.52 = bf16[64,8,48,128]{3,2,1,0:T(8,128)(2,1)} slice(bf16[64,8,128,128]{3,2,1,0:T(8,128)(2,1)} %bitcast.51), slice={[0:64], [0:8], [0:48], [0:128]} | slice | bytes 12582912 | tf_op jit(solution)/shard_map/slice | solution.py:268
  11.2 12.8 %all-to-all-start = ((bf16[64,8,48,128]{3,2,1,0:T(8,128)(2,1)}), bf16[64,8,48,128]{3,2,1,0:T(8,128)(2,1)}, u32[]{:S(2)}, u32[]{:S(2)}) async-start(bf16[64,8,48,128]{3,2,1,0:T(8,128)(2,1)} %slice.52), calls=%async_computation | async-start | bytes 12582912 | tf_op jit(solution)/shard_map/all_to_all | solution.py:235
  24.0 0.1 copy.18
  24.1 0.1 lt.20
  24.2 0.1 lt.23
  24.4 0.1 copy.19
  24.5 0.1 add.35
  24.7 0.1 copy.21
  24.8 11.7 %cholesky.44 = f32[128,128]{1,0:T(8,128)S(1)} custom-call(f32[128,128]{1,0:T(8,128)S(1)} %fusion.6), custom_call_target="Cholesky" | custom-call | tf_op jit(solution)/shard_map/jit(cholesky)/cholesky | solution.py:259
  36.5 0.6 compare_reduce_fusion.1
  37.2 0.7 select_bitcast_fusion.1
  37.8 9.8 %custom-call.6 = f32[1,128,128]{1,2,0:T(8,128)S(1)} custom-call(f32[1,128,128]{2,1,0:T(8,128)S(1)} %get-tuple-element.43), custom_call_target="InvertDiagBlocksLowerTriangular" | custom-call | tf_op jit(solution)/shard_map/jit(_solve_triangular)/triangular_solve | solution.py:240
  47.6 0.3 fusion.1
  47.9 0.1 copy.22
  48.0 0.2 convolution_convert_fusion.l21_ref
  48.3 0.1 slice_subtract_fusion
  48.4 0.1 copy.24
  48.6 11.7 %cholesky.55 = f32[128,128]{1,0:T(8,128)S(1)} custom-call(f32[128,128]{1,0:T(8,128)S(1)} %fusion.4), custom_call_target="Cholesky" | custom-call | tf_op jit(solution)/shard_map/jit(cholesky)/cholesky | solution.py:263
  60.3 0.6 compare_reduce_fusion
  61.0 0.7 select_bitcast_fusion
  61.6 10.0 %custom-call.7 = f32[1,128,128]{1,2,0:T(8,128)S(1)} custom-call(f32[1,128,128]{2,1,0:T(8,128)S(1)} %get-tuple-element.41), custom_call_target="InvertDiagBlocksLowerTriangular" | custom-call | tf_op jit(solution)/shard_map/jit(_solve_triangular)/triangular_solve | solution.py:240
  71.6 11.3 %slice.44 = bf16[64,8,80,128]{3,2,1,0:T(8,128)(2,1)} slice(bf16[64,8,128,128]{3,2,1,0:T(8,128)(2,1)} %bitcast.52), slice={[0:64], [0:8], [48:128], [0:128]} | slice | bytes 20971520 | tf_op jit(solution)/shard_map/slice | solution.py:270
  82.9 0.3 convolution_bitcast_fusion.t2_ref
  83.2 23.3 %all-to-all-done = bf16[64,8,48,128]{3,2,1,0:T(8,128)(2,1)} async-done(((bf16[64,8,48,128]{3,2,1,0:T(8,128)(2,1)}), bf16[64,8,48,128]{3,2,1,0:T(8,128)(2,1)}, u32[]{:S(2)}, u32[]{:S(2)}) %all-to-all-start) | async-done | bytes 6291488 | tf_op jit(solution)/shard_map/all_to_all | solution.py:235
  106.5 128.1 %all_to_all.10 = bf16[64,8,80,128]{3,2,1,0:T(8,128)(2,1)} all-to-all(bf16[64,8,80,128]{3,2,1,0:T(8,128)(2,1)} %slice.44), channel_id=1, replica_groups=mesh['group'=16,'row'=4,'col'=2] {'group','row'}, dimensions={0} | all-to-all | bytes 20971520 | tf_op jit(solution)/shard_map/all_to_all | solution.py:235
  234.6 3.7 %assemble.4 = (f32[40,128,256]{2,1,0:T(8,128)}, bf16[640,256]{1,0:T(8,128)(2,1)S(1)}) custom-call(s32[512]{0:T(512)S(1)} %broadcast_select_fusion.target, s32[2]{0:T(128)S(1)} %pad_add_fusion.place, bf16[512,48,128]{2,1,0:T(8,128)(2,1)} %bitcast.12.x_hbm, bf16[40,128,256]{2,1,0:T(8,128)(2,1)S(1)} %bitcast.41, f32[128,128]{1,0:T(8,128)S(1)} %bitcast.45, ...), custom_call_target="tpu_custom_call" | custom-call | flops 41943040 | bytes 2097152 | tf_op jit(solution)/shard_map/assemble/pallas_call | solution.py:117
  238.4 1.3 collective-permute-start.3
  239.7 5.1 %assemble.5 = (f32[40,128,256]{2,1,0:T(8,128)}, bf16[1280,256]{1,0:T(8,128)(2,1)S(1)}) custom-call(s32[512]{0:T(512)S(1)} %broadcast_select_fusion.target, s32[2]{0:T(128)S(1)} %pad_add_fusion.place, bf16[512,48,128]{2,1,0:T(8,128)(2,1)} %bitcast.12.x_hbm, bf16[40,128,256]{2,1,0:T(8,128)(2,1)S(1)} %bitcast.42, ...), custom_call_target="tpu_custom_call", output_to_operand_aliasing={{0}: (9, {})} | custom-call | flops 83886080 | bytes 4194304 | tf_op jit(solution)/shard_map/assemble/pallas_call | solution.py:117
  244.8 7.2 %collective-permute-done.3.refs_0_ = bf16[640,256]{1,0:T(8,128)(2,1)S(1)} collective-permute-done((bf16[640,256]{1,0:T(8,128)(2,1)S(1)}, bf16[640,256]{1,0:T(8,128)(2,1)S(1)}, u32[]{:S(2)}, u32[]{:S(2)}) %collective-permute-start.3) | collective-permute-done | bytes 327712 | tf_op jit(solution)/shard_map/ppermute | solution.py:292
  252.0 1.3 collective-permute-start.4
  253.3 6.7 %assemble.6 = (f32[40,128,256]{2,1,0:T(8,128)}, bf16[1920,256]{1,0:T(8,128)(2,1)S(1)}) custom-call(s32[512]{0:T(512)S(1)} %broadcast_select_fusion.target, s32[2]{0:T(128)S(1)} %pad_add_fusion.place, bf16[512,80,128]{2,1,0:T(8,128)(2,1)} %bitcast.49, bf16[40,128,256]{2,1,0:T(8,128)(2,1)S(1)} %bitcast.43, ...), custom_call_target="tpu_custom_call", output_to_operand_aliasing={{0}: (9, {})} | custom-call | flops 125829120 | bytes 6291456 | tf_op jit(solution)/shard_map/assemble/pallas_call | solution.py:117
  260.0 1.3 collective-permute-start.10
  261.3 11.7 %collective-permute-done.4.refs_1_ = bf16[1280,256]{1,0:T(8,128)(2,1)S(1)} collective-permute-done((bf16[1280,256]{1,0:T(8,128)(2,1)S(1)}, bf16[1280,256]{1,0:T(8,128)(2,1)S(1)}, u32[]{:S(2)}, u32[]{:S(2)}) %collective-permute-start.4) | collective-permute-done | bytes 655392 | tf_op jit(solution)/shard_map/ppermute | solution.py:292
  272.9 5.0 %assemble.7 = (f32[40,128,256]{2,1,0:T(8,128)}, bf16[1280,256]{1,0:T(8,128)(2,1)S(1)}) custom-call(s32[512]{0:T(512)S(1)} %broadcast_select_fusion.target, s32[2]{0:T(128)S(1)} %pad_add_fusion.place, bf16[512,80,128]{2,1,0:T(8,128)(2,1)} %bitcast.50, bf16[40,128,256]{2,1,0:T(8,128)(2,1)S(1)} %bitcast.44, ...), custom_call_target="tpu_custom_call", output_to_operand_aliasing={{0}: (9, {})} | custom-call | flops 83886080 | bytes 4194304 | tf_op jit(solution)/shard_map/assemble/pallas_call | solution.py:117
  278.0 0.7 collective-permute-start.8
  278.7 1.3 collective-permute-start.7
  280.0 0.7 collective-permute-start.6
  280.7 0.7 collective-permute-start.5
  281.3 14.7 %collective-permute-done.7 = bf16[256,256]{1,0:T(8,128)(2,1)S(1)} collective-permute-done((bf16[256,256]{1,0:T(8,128)(2,1)S(1)}, bf16[256,256]{1,0:T(8,128)(2,1)S(1)}, u32[]{:S(2)}, u32[]{:S(2)}) %collective-permute-start.7) | collective-permute-done | bytes 131104 | tf_op jit(solution)/shard_map/ppermute | solution.py:226
  296.1 1.3 collective-permute-start.9
  297.4 8.2 %update.2.refs_1_ = f32[40,128,256]{2,1,0:T(8,128)} custom-call(s32[2]{0:T(128)S(1)} %pad_add_fusion.place, bf16[256,256]{1,0:T(8,128)(2,1)S(1)} %add_add_fusion.p_hbm, bf16[640,256]{1,0:T(8,128)(2,1)S(1)} %collective-permute-done.3.refs_0_, bf16[1280,256]{1,0:T(8,128)(2,1)S(1)} %collective-permute-done.4.refs_1_, ...), custom_call_target="tpu_custom_call", output_to_operand_aliasing={{}: (5, {})} | custom-call | flops 503316480 | bytes 9830400 | tf_op jit(solution)/shard_map/update/pallas_call | solution.py:194
  305.6 8.9 %collective-permute-done.9.refs_0_ = bf16[1280,256]{1,0:T(8,128)(2,1)S(1)} collective-permute-done((bf16[1280,256]{1,0:T(8,128)(2,1)S(1)}, bf16[1280,256]{1,0:T(8,128)(2,1)S(1)}, u32[]{:S(2)}, u32[]{:S(2)}) %collective-permute-start.9) | collective-permute-done | bytes 655392 | tf_op jit(solution)/shard_map/ppermute | solution.py:292
  314.6 3.7 %update.3 = f32[40,128,256]{2,1,0:T(8,128)} custom-call(s32[2]{0:T(128)S(1)} %pad_add_fusion.place, bf16[256,256]{1,0:T(8,128)(2,1)S(1)} %add_add_fusion.p_hbm, bf16[1280,256]{1,0:T(8,128)(2,1)S(1)} %collective-permute-done.9.refs_0_, f32[40,128,256]{2,1,0:T(8,128)} %update.2.refs_1_), custom_call_target="tpu_custom_call", output_to_operand_aliasing={{}: (3, {})} | custom-call | flops 167772160 | bytes 3276800 | tf_op jit(solution)/shard_map/update/pallas_call | solution.py:194
  (31 shorter events, 0.4 us)
Async XLA Ops:
  1.0 10.1 %collective-permute-start.1 = (bf16[256,256]{0,1:T(8,128)(2,1)S(1)}, bf16[256,256]{0,1:T(8,128)(2,1)S(1)}, u32[]{:S(2)}, u32[]{:S(2)}) collective-permute-start(bf16[256,256]{0,1:T(8,128)(2,1)S(1)} %bitcast.53), channel_id=1, source_target_pairs={{0,4},{1,5},{8,12},{9,13},{16,20},{17,21},{24,28},{25,29},{32,36},... | collective-permute-start | bytes 393224 | tf_op jit(solution)/shard_map/ppermute | solution.py:226
  2.3 8.8 %collective-permute-start = (bf16[256,256]{0,1:T(8,128)(2,1)S(1)}, bf16[256,256]{0,1:T(8,128)(2,1)S(1)}, u32[]{:S(2)}, u32[]{:S(2)}) collective-permute-start(bf16[256,256]{0,1:T(8,128)(2,1)S(1)} %bitcast.54), channel_id=1, source_target_pairs={{0,2},{1,3},{8,10},{9,11},{16,18},{17,19},{24,26},{25,27},{32,34},... | collective-permute-start | bytes 393224 | tf_op jit(solution)/shard_map/ppermute | solution.py:226
  3.0 8.1 %collective-permute-start.2 = (bf16[256,256]{0,1:T(8,128)(2,1)S(1)}, bf16[256,256]{0,1:T(8,128)(2,1)S(1)}, u32[]{:S(2)}, u32[]{:S(2)}) collective-permute-start(bf16[256,256]{0,1:T(8,128)(2,1)S(1)} %bitcast.55), channel_id=1, source_target_pairs={{0,6},{1,7},{8,14},{9,15},{16,22},{17,23},{24,30},{25,31},{32,38},... | collective-permute-start | bytes 393224 | tf_op jit(solution)/shard_map/ppermute | solution.py:226
  11.2 12.8 %copy-start.3 = (s32[1,1,1,16,4]{3,4,2,1,0:T(4,128)S(1)}, s32[1,1,1,16,4]{3,4,2,1,0:T(4,128)}, u32[]{:S(2)}) copy-start(s32[1,1,1,16,4]{3,4,2,1,0:T(4,128)} %param.10) | copy-start | bytes 772
  11.2 13.2 %copy-start.1 = (s32[1,1,1,16,4,8]{3,5,4,2,1,0:T(8,128)S(1)}, s32[1,1,1,16,4,8]{3,5,4,2,1,0:T(8,128)}, u32[]{:S(2)}) copy-start(s32[1,1,1,16,4,8]{3,5,4,2,1,0:T(8,128)} %param.11) | copy-start | bytes 6148
  11.2 13.2 %copy-start.2 = (s32[1,1,1,16,4,8]{3,5,4,2,1,0:T(8,128)S(1)}, s32[1,1,1,16,4,8]{3,5,4,2,1,0:T(8,128)}, u32[]{:S(2)}) copy-start(s32[1,1,1,16,4,8]{3,5,4,2,1,0:T(8,128)} %param.12) | copy-start | bytes 6148
  11.2 95.3 %all-to-all-start = ((bf16[64,8,48,128]{3,2,1,0:T(8,128)(2,1)}), bf16[64,8,48,128]{3,2,1,0:T(8,128)(2,1)}, u32[]{:S(2)}, u32[]{:S(2)}) async-start(bf16[64,8,48,128]{3,2,1,0:T(8,128)(2,1)} %slice.52), calls=%async_computation | async-start | bytes 12582912 | tf_op jit(solution)/shard_map/all_to_all | solution.py:235
  106.5 128.1 %copy-start = (bf16[1,5120,256]{2,1,0:T(8,128)(2,1)S(1)}, bf16[1,5120,256]{2,1,0:T(8,128)(2,1)}, u32[]{:S(2)}) copy-start(bf16[1,5120,256]{2,1,0:T(8,128)(2,1)} %param.8) | copy-start | bytes 7864324
  238.4 13.6 %collective-permute-start.3 = (bf16[640,256]{1,0:T(8,128)(2,1)S(1)}, bf16[640,256]{1,0:T(8,128)(2,1)S(1)}, u32[]{:S(2)}, u32[]{:S(2)}) collective-permute-start(bf16[640,256]{1,0:T(8,128)(2,1)S(1)} %get-tuple-element.28), channel_id=1, source_target_pairs={{0,1},{2,3},{4,5},{6,7},{8,9},{10,11},{12,13},{14,15},{16,17},{18,... | collective-permute-start | bytes 983048 | tf_op jit(solution)/shard_map/ppermute | solution.py:292
  252.0 21.0 %collective-permute-start.4 = (bf16[1280,256]{1,0:T(8,128)(2,1)S(1)}, bf16[1280,256]{1,0:T(8,128)(2,1)S(1)}, u32[]{:S(2)}, u32[]{:S(2)}) collective-permute-start(bf16[1280,256]{1,0:T(8,128)(2,1)S(1)} %get-tuple-element.35), channel_id=1, source_target_pairs={{0,1},{2,3},{4,5},{6,7},{8,9},{10,11},{12,13},{14,15},{16,17},{18,... | collective-permute-start | bytes 1966088 | tf_op jit(solution)/shard_map/ppermute | solution.py:292
  260.0 37.4 %collective-permute-start.10 = (bf16[1920,256]{1,0:T(8,128)(2,1)S(1)}, bf16[1920,256]{1,0:T(8,128)(2,1)S(1)}, u32[]{:S(2)}, u32[]{:S(2)}) collective-permute-start(bf16[1920,256]{1,0:T(8,128)(2,1)S(1)} %get-tuple-element.34), channel_id=1, source_target_pairs={{0,1},{2,3},{4,5},{6,7},{8,9},{10,11},{12,13},{14,15},{16,17},{18,... | collective-permute-start | bytes 2949128 | tf_op jit(solution)/shard_map/ppermute | solution.py:292
  278.0 3.3 %collective-permute-start.8 = (bf16[256,256]{1,0:T(8,128)(2,1)S(1)}, bf16[256,256]{1,0:T(8,128)(2,1)S(1)}, u32[]{:S(2)}, u32[]{:S(2)}) collective-permute-start(bf16[256,256]{1,0:T(8,128)(2,1)S(1)} %bitcast.57), channel_id=1, source_target_pairs={{0,7},{8,15},{16,23},{24,31},{32,39},{40,47},{48,55},{56,63},{64,7... | collective-permute-start | bytes 393224 | tf_op jit(solution)/shard_map/ppermute | solution.py:226
  278.7 17.4 %collective-permute-start.7 = (bf16[256,256]{1,0:T(8,128)(2,1)S(1)}, bf16[256,256]{1,0:T(8,128)(2,1)S(1)}, u32[]{:S(2)}, u32[]{:S(2)}) collective-permute-start(bf16[256,256]{1,0:T(8,128)(2,1)S(1)} %bitcast.58), channel_id=1, source_target_pairs={{0,5},{8,13},{16,21},{24,29},{32,37},{40,45},{48,53},{56,61},{64,6... | collective-permute-start | bytes 393224 | tf_op jit(solution)/shard_map/ppermute | solution.py:226
  280.0 16.1 %collective-permute-start.6 = (bf16[256,256]{1,0:T(8,128)(2,1)S(1)}, bf16[256,256]{1,0:T(8,128)(2,1)S(1)}, u32[]{:S(2)}, u32[]{:S(2)}) collective-permute-start(bf16[256,256]{1,0:T(8,128)(2,1)S(1)} %bitcast.59), channel_id=1, source_target_pairs={{0,3},{8,11},{16,19},{24,27},{32,35},{40,43},{48,51},{56,59},{64,6... | collective-permute-start | bytes 393224 | tf_op jit(solution)/shard_map/ppermute | solution.py:226
  280.7 15.4 %collective-permute-start.5 = (bf16[256,256]{1,0:T(8,128)(2,1)S(1)}, bf16[256,256]{1,0:T(8,128)(2,1)S(1)}, u32[]{:S(2)}, u32[]{:S(2)}) collective-permute-start(bf16[256,256]{1,0:T(8,128)(2,1)S(1)} %bitcast.60), channel_id=1, source_target_pairs={{0,1},{8,9},{16,17},{24,25},{32,33},{40,41},{48,49},{56,57},{64,65... | collective-permute-start | bytes 393224 | tf_op jit(solution)/shard_map/ppermute | solution.py:226
  296.1 18.5 %collective-permute-start.9 = (bf16[1280,256]{1,0:T(8,128)(2,1)S(1)}, bf16[1280,256]{1,0:T(8,128)(2,1)S(1)}, u32[]{:S(2)}, u32[]{:S(2)}) collective-permute-start(bf16[1280,256]{1,0:T(8,128)(2,1)S(1)} %get-tuple-element.39), channel_id=1, source_target_pairs={{0,1},{2,3},{4,5},{6,7},{8,9},{10,11},{12,13},{14,15},{16,17},{18,... | collective-permute-start | bytes 1966088 | tf_op jit(solution)/shard_map/ppermute | solution.py:292

commit v3 on v2

--- a/solution.py
+++ b/solution.py
@@ -8,21 +8,101 @@
 from jax.sharding import PartitionSpec as P
 
 PB = 128
-CHUNKS = (48, 80)
-PIECES = ((0, 0, 16), (0, 16, 32), (1, 0, 48), (1, 48, 32))
+PIECES = (32, 64, 32)
 CHAINS = 4
 DEPTH = 4
 BLOCK = 64
+PIVOTS = 4
 EXACT = lax.Precision.HIGHEST
 VMEM = pl.BlockSpec(memory_space=pltpu.VMEM)
 
 
-def dot_t(a, b):
-    return lax.dot_general(a, b, (((1,), (1,)), ((), ())), preferred_element_type=jnp.float32)
+def dot_t(a, b, precision=None):
+    return lax.dot_general(
+        a, b, (((1,), (1,)), ((), ())), precision=precision, preferred_element_type=jnp.float32
+    )
+
+
+def split(x):
+    high = x.astype(jnp.bfloat16)
+    return high, (x - high.astype(jnp.float32)).astype(jnp.bfloat16)
+
+
+def paired(x):
+    high, low = split(x)
+    return jnp.concatenate([high, low, high], axis=1)
+
+
+def solve(x, inverse):
+    high, low = split(x)
+    return dot_t(jnp.concatenate([high, high, low], axis=1), inverse)
+
+
+def eliminate(block, raw_ref, unit_ref):
+    lane = lax.broadcasted_iota(jnp.int32, (8, PB), 1)
+    line = lax.broadcasted_iota(jnp.int32, (8, PB), 0)
+    n = PB // 8
+    m = [block[8 * k : 8 * k + 8] for k in range(n)]
+    for first in range(0, PB, PIVOTS):
+        b, s = divmod(first, 8)
+        cols = {
+            k: [jnp.broadcast_to(m[k][:, first + c : first + c + 1], (8, PB)) for c in range(PIVOTS)]
+            for k in range(b, n)
+        }
+        for c in range(PIVOTS):
+            j, own = first + c, s + c
+            inverse = 1.0 / cols[b][c][own : own + 1]
+            here = lane == j
+            pivot = jnp.where(here[:1], 1.0, m[b][own : own + 1]) * inverse
+            factors = [cols[b][e][own : own + 1] * inverse for e in range(c + 1, PIVOTS)]
+            for k in range(b, n):
+                col = cols[k][c]
+                raw_ref[8 * k : 8 * k + 8, j : j + 1] = col[:, j : j + 1]
+                new = jnp.where(here, 0.0, m[k]) - col * pivot
+                m[k] = new if k > b else jnp.where(line > own, new, m[k])
+                for e in range(c + 1, PIVOTS):
+                    new = cols[k][e] - col * factors[e - c - 1]
+                    cols[k][e] = new if k > b else jnp.where(line > own, new, cols[k][e])
+    for k in range(n):
+        unit_ref[8 * k : 8 * k + 8] = m[k]
+    line = lax.broadcasted_iota(jnp.int32, (PB, PB), 0)
+    lane = lax.broadcasted_iota(jnp.int32, (PB, PB), 1)
+    raw = raw_ref[...]
+    diagonal = jnp.where(line == lane, raw, 0.0)
+    factor = raw / jnp.sqrt(jnp.sum(diagonal, axis=0, keepdims=True))
+    unit = jnp.where(line > lane, unit_ref[...], jnp.where(line == lane, 1.0, 0.0))
+    inverse = unit / jnp.sqrt(jnp.sum(diagonal, axis=1, keepdims=True))
+    return jnp.where(line >= lane, factor, 0.0), inverse
+
+
+def factor_kernel(lead_ref, l11_ref, i1_ref, l21_ref, l22_ref, i2_ref, raw_ref, unit_ref):
+    def symmetric(block):
+        return (block + block.T) * 0.5
+
+    lead = lead_ref[...].astype(jnp.float32)
+    factor, inverse = eliminate(symmetric(lead[:PB, :PB]), raw_ref, unit_ref)
+    l11_ref[...], i1_ref[...] = factor, paired(inverse)
+    l21 = dot_t(lead[PB:, :PB], inverse, EXACT).astype(jnp.bfloat16)
+    l21_ref[...] = l21
+    rest = symmetric(lead[PB:, PB:]) - dot_t(l21, l21)
+    l22_ref[...], inverse = eliminate(rest, raw_ref, unit_ref)
+    i2_ref[...] = paired(inverse)
+
+
+def factor_lead(lead):
+    square = jax.ShapeDtypeStruct((PB, PB), jnp.float32)
+    wide = jax.ShapeDtypeStruct((PB, 3 * PB), jnp.bfloat16)
+    return pl.pallas_call(
+        factor_kernel,
+        out_shape=[square, wide, jax.ShapeDtypeStruct((PB, PB), jnp.bfloat16), square, wide],
+        scratch_shapes=[pltpu.VMEM((PB, PB), jnp.float32)] * 2,
+        compiler_params=pltpu.CompilerParams(vmem_limit_bytes=16 * 1024 * 1024),
+        name="factor",
+    )(lead)
 
 
 def assemble_kernel(
-    rows, offset, start, target, place, x_hbm, e_hbm, t1_ref, t2_ref, l21_ref, l11_ref, l22_ref, *refs
+    rows, offset, start, target, place, x_hbm, e_hbm, i1_ref, i2_ref, l21_ref, l11_ref, l22_ref, *refs
 ):
     f_hbm, h_hbm, x_ref, e_ref, f_ref, h_ref, x_sem, e_sem, f_sem, h_sem = refs[-CHAINS - 10 : -CHAINS]
     acc = refs[-CHAINS:]
@@ -83,13 +163,13 @@
 
         @pl.when(place[1] == 0)
         def _():
-            x1 = jnp.dot(left, t1_ref[...], precision=EXACT, preferred_element_type=jnp.float32)
+            x1 = solve(left, i1_ref[...])
             if g == 0:
                 top = jnp.concatenate([l11_ref[here, :], x1[rows:]], axis=0)
                 x1 = jnp.where(place[0] == 0, top, x1)
             h1 = x1.astype(jnp.bfloat16)
             right2 = right - dot_t(h1, l21_ref[...])
-            x2 = jnp.dot(right2, t2_ref[...], precision=EXACT, preferred_element_type=jnp.float32)
+            x2 = solve(right2, i2_ref[...])
             if g == 0:
                 top = [jnp.zeros((rows, PB), jnp.float32), l22_ref[here, :], x2[2 * rows :]]
                 x2 = jnp.where(place[0] == 0, jnp.concatenate(top, axis=0), x2)
@@ -106,11 +186,11 @@
         copy.wait()
 
 
-def assemble(target, place, received, offset, entries, start, rows, t1, t2, l21, l11, l22, base):
+def assemble(target, place, received, offset, entries, start, rows, i1, i2, l21, l11, l22, base):
     slots = received.shape[0]
     tiles = entries.shape[0]
     anywhere = pl.BlockSpec(memory_space=pl.ANY)
-    square = pl.BlockSpec((PB, PB), lambda i, *_: (0, 0))
+    whole = lambda x: pl.BlockSpec(x.shape, lambda i, *_: (0, 0))
     extra = [] if base is None else [base]
     front = jax.ShapeDtypeStruct((tiles, PB, 2 * PB), jnp.float32)
     half = jax.ShapeDtypeStruct((tiles * rows, 2 * PB), jnp.bfloat16)
@@ -119,7 +199,7 @@
         grid_spec=pltpu.PrefetchScalarGridSpec(
             num_scalar_prefetch=2,
             grid=(1,),
-            in_specs=[anywhere, anywhere] + [square] * 5 + [anywhere] * len(extra),
+            in_specs=[anywhere, anywhere] + [whole(x) for x in (i1, i2, l21, l11, l22)] + [anywhere] * len(extra),
             out_specs=[anywhere, anywhere],
             scratch_shapes=[
                 pltpu.VMEM((slots, rows, PB), jnp.bfloat16),
@@ -142,7 +222,7 @@
             flops=slots * rows * PB * 40, bytes_accessed=slots * rows * PB * 2, transcendentals=0
         ),
         name="assemble",
-    )(target, place, received, entries, t1, t2, l21, l11, l22, *extra)
+    )(target, place, received, entries, i1, i2, l21, l11, l22, *extra)
 
 
 def update_kernel(pieces, place, p_hbm, *refs):
@@ -235,11 +315,6 @@
     return lax.all_to_all(x, ("group", "row"), split_axis=0, concat_axis=0, tiled=True)
 
 
-def inverse_t(factor):
-    eye = jnp.eye(PB, dtype=jnp.float32)
-    return jax.scipy.linalg.solve_triangular(factor, eye, lower=True).T
-
-
 def local(front_entries, contrib, counts, tile_rows, tile_cols):
     entries = front_entries[0]
     row, col = lax.axis_index("row"), lax.axis_index("col")
@@ -255,38 +330,28 @@
     lead = entries[: 2 * PB]
     lead = from_first(
         lead, "row", (1, 2, 3), jnp.where(row == 0, lead, jnp.zeros_like(lead))
-    ).astype(jnp.float32)
-    l11 = jnp.linalg.cholesky(lead[:PB, :PB])
-    t1 = inverse_t(l11)
-    l21 = jnp.dot(lead[PB:, :PB], t1, precision=EXACT).astype(jnp.bfloat16)
-    rest = lead[PB:, PB:] - dot_t(l21, l21)
-    l22 = jnp.linalg.cholesky(rest)
-    t2 = inverse_t(l22)
-
+    )
+    l11, i1, l21, l22, i2 = factor_lead(lead)
     shaped = entries.reshape(tiles, PB, 2 * PB)
-    ready = (target, place, t1, t2, l11, l21, l22)
-    piece = after(outgoing[:, :, : CHUNKS[0]], lead)
-    first = exchange(piece)
-    piece = after(outgoing, piece)[:, :, CHUNKS[0] :]
-    first, second = lax.optimization_barrier((first, exchange(after(piece, (first, ready)))))
-    received = [r.reshape(owners * slots, -1, PB) for r in (first, second)]
+    ready = (target, place, i1, i2, l11, l21, l22)
+    received = exchange(after(outgoing, ready)).reshape(owners * slots, PB, PB)
 
     halves, columns, rows_of = [], [], []
     front, start = None, 0
-    for chunk, offset, rows in PIECES:
-        tiles_in = received[chunk]
-        if len(halves) >= 2:
-            tiles_in = after(tiles_in, halves[-2])
+    for rows in PIECES:
+        source = after(received, halves[-2]) if len(halves) >= 2 else received
         front, h = assemble(
-            target, place, tiles_in, offset, shaped, start, rows, t1, t2, l21, l11, l22, front
+            target, place, source, start, shaped, start, rows, i1, i2, l21, l11, l22, front
         )
         columns.append(h[2 * rows : 4 * rows].reshape(2, rows, 2 * PB))
         rows_of.append((start, rows))
         start += rows
         if start == PB:
             columns = jnp.concatenate(columns, axis=1).reshape(2 * PB, 2 * PB)
-            columns = from_first(columns, ("row", "col"), (1, 3, 5, 7), jnp.zeros_like(columns))
-            h = after(h, columns)
+            near = [lax.ppermute(columns, ("row", "col"), [(0, t)]) for t in (1, 5)]
+            near = near[0] + near[1]
+            h = after(h, near)
+            columns = near + lax.ppermute(near, ("row", "col"), [(1, 3), (5, 7)])
         if len(halves) == 1:
             h = after(h, halves[0])
         halves.append(lax.ppermute(h, "col", [(0, 1)]))

time: 320 us -> 303 us (0.947)
  blocking collectives: 128 us -> 198 us
  other arithmetic: 46.2 us -> 1.93 us
  local copies, waits for them, and re-layouts: 20.5 us -> 2.06 us
  starting transfers between devices: 23.9 us -> 9.75 us
  waiting for transfers between devices: 65.9 us -> 55.2 us
    all_to_all x1, blocking collectives: 128 us -> 198 us  [exchange(): lax.all_to_all(x, ('group', 'row'), split_axis=0, concat_axis=0, tiled=True)]
    another operation x10 -> x0, other arithmetic: 45.9 us -> none  [the longest x4 21.1 us: inverse_t(): return jax.scipy.linalg.solve_triangular(factor, eye, lower=True).T]
    ppermute x0 -> x3, waiting for transfers between devices: none -> 35.3 us  [the longest x2 34.3 us: local(): near = [lax.ppermute(columns, ('row', 'col'), [(0, t)]) for t in (1, 5)]]
    all_to_all x1 -> x0, waiting for transfers between devices: 23.3 us -> none  [exchange(): lax.all_to_all(x, ('group', 'row'), split_axis=0, concat_axis=0, tiled=True)]
    slice x4 -> x0, local copies, waits for them, and re-layouts: 18.8 us -> none  [the longest x1 11.3 us: local(): piece = after(outgoing, piece)[:, :, CHUNKS[0]:]]
    all_to_all x1 -> x0, starting transfers between devices: 12.8 us -> none  [exchange(): lax.all_to_all(x, ('group', 'row'), split_axis=0, concat_axis=0, tiled=True)]
    ppermute x7 -> x3, waiting for transfers between devices: 14.7 us -> 2.15 us  [from_first(): total = total + lax.ppermute(x, axes, [(0, t)])]
    ppermute x4 -> x3, waiting for transfers between devices: 27.8 us -> 17.8 us  [local(): halves.append(lax.ppermute(h, 'col', [(0, 1)]))]
  transfers between devices with their start and end apart: 12 -> 9, of which waited for: 5 -> 5; matrix products, arithmetic and copies ran while one was open for 21% -> 1% of each run, Pallas kernels for 8% -> 6%
where the time goes in v3:
time: 303 us
  blocking collectives  198 us (65%)
  waiting for transfers between devices  55.2 us (18%)
  Pallas kernels  35.4 us (12%)
  starting transfers between devices  9.75 us (3%)
    all_to_all x1, blocking collectives, exchange(): lax.all_to_all(x, ('group', 'row'), split_axis=0, concat_axis=0, tiled=True)  198 us
    ppermute x2, waiting for transfers between devices, local(): near = [lax.ppermute(columns, ('row', 'col'), [(0, t)]) for t in (1, 5)]  34.3 us
    ppermute x3, waiting for transfers between devices, local(): halves.append(lax.ppermute(h, 'col', [(0, 1)]))  17.8 us
    pallas_call x3, Pallas kernels, assemble(): pl.pallas_call(functools.partial(assemble_kernel, rows, offset, start), g...  16.4 us
    pallas_call x1, Pallas kernels, factor_lead(): pl.pallas_call(factor_kernel, out_shape=[square, wide, jax.ShapeDtypeStru...  9.67 us
    pallas_call x2, Pallas kernels, update(): pl.pallas_call(functools.partial(update_kernel, pieces), grid_spec=pltpu....  9.35 us
  transfers between devices with their start and end apart: 9, of which 5 were waited for; matrix products, arithmetic and copies ran while one was open for 1% of the time, Pallas kernels for 6%

profile of v3, /device:TPU:14, one launch (start us, length us, event | category | flops | bytes accessed | tf_op | source)
XLA Modules:
  0.0 302.5 jit_solution(2683949063481198174)
XLA Ops:
  0.0 0.9 slice_bitcast_fusion
  0.9 1.3 collective-permute-start.1
  2.2 0.7 collective-permute-start
  2.9 0.7 collective-permute-start.2
  3.6 0.8 copy.11
  4.3 0.1 lt.20
  4.4 0.1 iota_compare_fusion
  4.5 0.1 lt.23
  4.6 0.7 multiply_add_fusion
  5.4 0.1 copy.12
  5.4 0.1 add.23
  5.6 0.1 pad_add_fusion.place
  5.6 2.1 collective-permute-done.1
  7.8 0.0 collective-permute-done
  7.8 0.0 collective-permute-done.2
  7.8 0.9 add_add_fusion.lead_ref
  8.7 9.7 %factor.1 = (f32[128,128]{1,0:T(8,128)S(1)}, bf16[128,384]{1,0:T(8,128)(2,1)S(1)}, bf16[128,128]{1,0:T(8,128)(2,1)S(1)}, f32[128,128]{1,0:T(8,128)S(1)}, bf16[128,384]{1,0:T(8,128)(2,1)S(1)}) custom-call(bf16[256,256]{1,0:T(8,128)(2,1)S(1)} %add_add_fusion.lead_ref), custom_call_target="tpu_custom_call" | custom-call | tf_op jit(solution)/shard_map/factor/pallas_call | solution.py:95
  18.4 0.0 copy-start
  18.4 197.8 %all_to_all.5 = bf16[64,8,128,128]{3,2,1,0:T(8,128)(2,1)} all-to-all(bf16[64,8,128,128]{3,2,1,0:T(8,128)(2,1)} %bitcast.22), channel_id=1, replica_groups=mesh['group'=16,'row'=4,'col'=2] {'group','row'}, dimensions={0} | all-to-all | bytes 33554432 | tf_op jit(solution)/shard_map/all_to_all | solution.py:315
  216.2 0.0 copy-done
  216.2 5.0 %assemble.3 = (f32[40,128,256]{2,1,0:T(8,128)}, bf16[1280,256]{1,0:T(8,128)(2,1)S(1)}) custom-call(s32[512]{0:T(512)S(1)} %broadcast_select_fusion.target, s32[2]{0:T(128)S(1)} %pad_add_fusion.place, bf16[512,128,128]{2,1,0:T(8,128)(2,1)} %bitcast.19, bf16[40,128,256]{2,1,0:T(8,128)(2,1)S(1)} %bitcast.16, bf16[128,384]{1,0:T(8,128)(2,1)S(1)} %get-tuple-element.20.i1_ref, ...), custom_call_target="tpu_custom_call" | custom-call | flops 83886080 | bytes 4194304 | tf_op jit(solution)/shard_map/assemble/pallas_call | solution.py:197
  221.2 1.3 collective-permute-start.3
  222.5 6.4 %assemble.4 = (f32[40,128,256]{2,1,0:T(8,128)}, bf16[2560,256]{1,0:T(8,128)(2,1)S(1)}) custom-call(s32[512]{0:T(512)S(1)} %broadcast_select_fusion.target, s32[2]{0:T(128)S(1)} %pad_add_fusion.place, bf16[512,128,128]{2,1,0:T(8,128)(2,1)} %bitcast.20, bf16[40,128,256]{2,1,0:T(8,128)(2,1)S(1)} %bitcast.17, ...), custom_call_target="tpu_custom_call", output_to_operand_aliasing={{0}: (9, {})} | custom-call | flops 167772160 | bytes 8388608 | tf_op jit(solution)/shard_map/assemble/pallas_call | solution.py:197
  228.9 13.0 %collective-permute-done.3.refs_0_ = bf16[1280,256]{1,0:T(8,128)(2,1)S(1)} collective-permute-done((bf16[1280,256]{1,0:T(8,128)(2,1)S(1)}, bf16[1280,256]{1,0:T(8,128)(2,1)S(1)}, u32[]{:S(2)}, u32[]{:S(2)}) %collective-permute-start.3) | collective-permute-done | bytes 655392 | tf_op jit(solution)/shard_map/ppermute | solution.py:357
  242.0 1.3 collective-permute-start.8
  243.3 5.0 %assemble.5 = (f32[40,128,256]{2,1,0:T(8,128)}, bf16[1280,256]{1,0:T(8,128)(2,1)S(1)}) custom-call(s32[512]{0:T(512)S(1)} %broadcast_select_fusion.target, s32[2]{0:T(128)S(1)} %pad_add_fusion.place, bf16[512,128,128]{2,1,0:T(8,128)(2,1)} %bitcast.21, bf16[40,128,256]{2,1,0:T(8,128)(2,1)S(1)} %bitcast.18, ...), custom_call_target="tpu_custom_call", output_to_operand_aliasing={{0}: (9, {})} | custom-call | flops 83886080 | bytes 4194304 | tf_op jit(solution)/shard_map/assemble/pallas_call | solution.py:197
  248.3 1.3 collective-permute-start.5
  249.6 0.7 collective-permute-start.4
  250.3 34.3 %collective-permute-done.5 = bf16[256,256]{1,0:T(8,128)(2,1)S(1)} collective-permute-done((bf16[256,256]{1,0:T(8,128)(2,1)S(1)}, bf16[256,256]{1,0:T(8,128)(2,1)S(1)}, u32[]{:S(2)}, u32[]{:S(2)}) %collective-permute-start.5) | collective-permute-done | bytes 131104 | tf_op jit(solution)/shard_map/ppermute | solution.py:351
  284.6 0.0 collective-permute-done.4
  284.6 1.3 collective-permute-start.7
  285.9 1.3 collective-permute-start.6
  287.2 1.0 collective-permute-done.6
  288.2 0.0 collective-permute-done.8.refs_1_
  288.2 5.6 %update.2.refs_1_ = f32[40,128,256]{2,1,0:T(8,128)} custom-call(s32[2]{0:T(128)S(1)} %pad_add_fusion.place, bf16[256,256]{1,0:T(8,128)(2,1)S(1)} %add.28.p_hbm, bf16[1280,256]{1,0:T(8,128)(2,1)S(1)} %collective-permute-done.3.refs_0_, bf16[2560,256]{1,0:T(8,128)(2,1)S(1)} %collective-permute-done.8.refs_1_, ...), custom_call_target="tpu_custom_call", output_to_operand_aliasing={{}: (4, {})} | custom-call | flops 503316480 | bytes 9830400 | tf_op jit(solution)/shard_map/update/pallas_call | solution.py:274
  293.8 4.8 %collective-permute-done.7.refs_0_ = bf16[1280,256]{1,0:T(8,128)(2,1)S(1)} collective-permute-done((bf16[1280,256]{1,0:T(8,128)(2,1)S(1)}, bf16[1280,256]{1,0:T(8,128)(2,1)S(1)}, u32[]{:S(2)}, u32[]{:S(2)}) %collective-permute-start.7) | collective-permute-done | bytes 655392 | tf_op jit(solution)/shard_map/ppermute | solution.py:357
  298.6 3.7 %update.3 = f32[40,128,256]{2,1,0:T(8,128)} custom-call(s32[2]{0:T(128)S(1)} %pad_add_fusion.place, bf16[256,256]{1,0:T(8,128)(2,1)S(1)} %add.28.p_hbm, bf16[1280,256]{1,0:T(8,128)(2,1)S(1)} %collective-permute-done.7.refs_0_, f32[40,128,256]{2,1,0:T(8,128)} %update.2.refs_1_), custom_call_target="tpu_custom_call", output_to_operand_aliasing={{}: (3, {})} | custom-call | flops 167772160 | bytes 3276800 | tf_op jit(solution)/shard_map/update/pallas_call | solution.py:274
  (7 shorter events, 0.1 us)
Async XLA Ops:
  0.9 6.9 %collective-permute-start.1 = (bf16[256,256]{1,0:T(8,128)(2,1)S(1)}, bf16[256,256]{1,0:T(8,128)(2,1)S(1)}, u32[]{:S(2)}, u32[]{:S(2)}) collective-permute-start(bf16[256,256]{1,0:T(8,128)(2,1)S(1)} %slice_bitcast_fusion), channel_id=1, source_target_pairs={{0,4},{1,5},{8,12},{9,13},{16,20},{17,21},{24,28},{25,29},{32,36},... | collective-permute-start | bytes 393224 | tf_op jit(solution)/shard_map/ppermute | solution.py:306
  2.2 5.6 %collective-permute-start = (bf16[256,256]{1,0:T(8,128)(2,1)S(1)}, bf16[256,256]{1,0:T(8,128)(2,1)S(1)}, u32[]{:S(2)}, u32[]{:S(2)}) collective-permute-start(bf16[256,256]{1,0:T(8,128)(2,1)S(1)} %slice_bitcast_fusion), channel_id=1, source_target_pairs={{0,2},{1,3},{8,10},{9,11},{16,18},{17,19},{24,26},{25,27},{32,34},... | collective-permute-start | bytes 393224 | tf_op jit(solution)/shard_map/ppermute | solution.py:306
  2.9 4.9 %collective-permute-start.2 = (bf16[256,256]{1,0:T(8,128)(2,1)S(1)}, bf16[256,256]{1,0:T(8,128)(2,1)S(1)}, u32[]{:S(2)}, u32[]{:S(2)}) collective-permute-start(bf16[256,256]{1,0:T(8,128)(2,1)S(1)} %slice_bitcast_fusion), channel_id=1, source_target_pairs={{0,6},{1,7},{8,14},{9,15},{16,22},{17,23},{24,30},{25,31},{32,38},... | collective-permute-start | bytes 393224 | tf_op jit(solution)/shard_map/ppermute | solution.py:306
  18.4 197.8 %copy-start = (bf16[1,5120,256]{2,1,0:T(8,128)(2,1)S(1)}, bf16[1,5120,256]{2,1,0:T(8,128)(2,1)}, u32[]{:S(2)}) copy-start(bf16[1,5120,256]{2,1,0:T(8,128)(2,1)} %param.5) | copy-start | bytes 7864324
  221.2 20.8 %collective-permute-start.3 = (bf16[1280,256]{1,0:T(8,128)(2,1)S(1)}, bf16[1280,256]{1,0:T(8,128)(2,1)S(1)}, u32[]{:S(2)}, u32[]{:S(2)}) collective-permute-start(bf16[1280,256]{1,0:T(8,128)(2,1)S(1)} %get-tuple-element.26), channel_id=1, source_target_pairs={{0,1},{2,3},{4,5},{6,7},{8,9},{10,11},{12,13},{14,15},{16,17},{18,... | collective-permute-start | bytes 1966088 | tf_op jit(solution)/shard_map/ppermute | solution.py:357
  242.0 46.3 %collective-permute-start.8 = (bf16[2560,256]{1,0:T(8,128)(2,1)S(1)}, bf16[2560,256]{1,0:T(8,128)(2,1)S(1)}, u32[]{:S(2)}, u32[]{:S(2)}) collective-permute-start(bf16[2560,256]{1,0:T(8,128)(2,1)S(1)} %get-tuple-element.33), channel_id=1, source_target_pairs={{0,1},{2,3},{4,5},{6,7},{8,9},{10,11},{12,13},{14,15},{16,17},{18,... | collective-permute-start | bytes 3932168 | tf_op jit(solution)/shard_map/ppermute | solution.py:357
  248.3 36.3 %collective-permute-start.5 = (bf16[256,256]{1,0:T(8,128)(2,1)S(1)}, bf16[256,256]{1,0:T(8,128)(2,1)S(1)}, u32[]{:S(2)}, u32[]{:S(2)}) collective-permute-start(bf16[256,256]{1,0:T(8,128)(2,1)S(1)} %bitcast.24), channel_id=1, source_target_pairs={{0,5},{8,13},{16,21},{24,29},{32,37},{40,45},{48,53},{56,61},{64,6... | collective-permute-start | bytes 393224 | tf_op jit(solution)/shard_map/ppermute | solution.py:351
  249.6 35.0 %collective-permute-start.4 = (bf16[256,256]{1,0:T(8,128)(2,1)S(1)}, bf16[256,256]{1,0:T(8,128)(2,1)S(1)}, u32[]{:S(2)}, u32[]{:S(2)}) collective-permute-start(bf16[256,256]{1,0:T(8,128)(2,1)S(1)} %bitcast.25), channel_id=1, source_target_pairs={{0,1},{8,9},{16,17},{24,25},{32,33},{40,41},{48,49},{56,57},{64,65... | collective-permute-start | bytes 393224 | tf_op jit(solution)/shard_map/ppermute | solution.py:351
  284.6 14.0 %collective-permute-start.7 = (bf16[1280,256]{1,0:T(8,128)(2,1)S(1)}, bf16[1280,256]{1,0:T(8,128)(2,1)S(1)}, u32[]{:S(2)}, u32[]{:S(2)}) collective-permute-start(bf16[1280,256]{1,0:T(8,128)(2,1)S(1)} %get-tuple-element.32), channel_id=1, source_target_pairs={{0,1},{2,3},{4,5},{6,7},{8,9},{10,11},{12,13},{14,15},{16,17},{18,... | collective-permute-start | bytes 1966088 | tf_op jit(solution)/shard_map/ppermute | solution.py:357
  285.9 2.3 collective-permute-start.6

commit v4 on v3

--- a/solution.py
+++ b/solution.py
@@ -339,7 +339,11 @@
     halves, columns, rows_of = [], [], []
     front, start = None, 0
     for rows in PIECES:
-        source = after(received, halves[-2]) if len(halves) >= 2 else received
+        source = received
+        if len(halves) >= 1:
+            source = after(source, h)
+        if len(halves) >= 2:
+            source = after(source, halves[-2])
         front, h = assemble(
             target, place, source, start, shaped, start, rows, i1, i2, l21, l11, l22, front
         )
@@ -352,8 +356,6 @@
             near = near[0] + near[1]
             h = after(h, near)
             columns = near + lax.ppermute(near, ("row", "col"), [(1, 3), (5, 7)])
-        if len(halves) == 1:
-            h = after(h, halves[0])
         halves.append(lax.ppermute(h, "col", [(0, 1)]))
     front = update(place, front, halves[:-1], rows_of[:-1], columns)
     front = update(place, front, halves[-1:], rows_of[-1:], columns)

time: 303 us -> 297 us (0.980)
  waiting for transfers between devices: 55.2 us -> 49.3 us
    ppermute x2, waiting for transfers between devices: 34.3 us -> 29.7 us  [local(): near = [lax.ppermute(columns, ('row', 'col'), [(0, t)]) for t in (1, 5)]]
where the time goes in v4:
time: 297 us
  blocking collectives  198 us (67%)
  waiting for transfers between devices  49.3 us (17%)
  Pallas kernels  35.4 us (12%)
  starting transfers between devices  9.76 us (3%)
    all_to_all x1, blocking collectives, exchange(): lax.all_to_all(x, ('group', 'row'), split_axis=0, concat_axis=0, tiled=True)  198 us
    ppermute x2, waiting for transfers between devices, local(): near = [lax.ppermute(columns, ('row', 'col'), [(0, t)]) for t in (1, 5)]  29.7 us
    ppermute x3, waiting for transfers between devices, local(): halves.append(lax.ppermute(h, 'col', [(0, 1)]))  16.5 us
    pallas_call x3, Pallas kernels, assemble(): pl.pallas_call(functools.partial(assemble_kernel, rows, offset, start), g...  16.4 us
    pallas_call x1, Pallas kernels, factor_lead(): pl.pallas_call(factor_kernel, out_shape=[square, wide, jax.ShapeDtypeStru...  9.67 us
    pallas_call x2, Pallas kernels, update(): pl.pallas_call(functools.partial(update_kernel, pieces), grid_spec=pltpu....  9.35 us
  transfers between devices with their start and end apart: 9, of which 5 were waited for; matrix products, arithmetic and copies ran while one was open for 1% of the time, Pallas kernels for 6%

profile of v4, /device:TPU:14, one launch (start us, length us, event | category | flops | bytes accessed | tf_op | source)
XLA Modules:
  0.0 296.6 jit_solution(14165841063855701144)
XLA Ops:
  0.0 0.9 slice_bitcast_fusion
  0.9 1.3 collective-permute-start.1
  2.2 0.7 collective-permute-start
  2.9 0.7 collective-permute-start.2
  3.6 0.8 copy.11
  4.3 0.1 lt.20
  4.4 0.1 iota_compare_fusion
  4.5 0.1 lt.23
  4.6 0.7 multiply_add_fusion
  5.4 0.1 copy.12
  5.4 0.1 add.23
  5.6 0.1 pad_add_fusion.place
  5.6 2.1 collective-permute-done.1
  7.8 0.0 collective-permute-done
  7.8 0.0 collective-permute-done.2
  7.8 0.9 add_add_fusion.lead_ref
  8.7 9.7 %factor.1 = (f32[128,128]{1,0:T(8,128)S(1)}, bf16[128,384]{1,0:T(8,128)(2,1)S(1)}, bf16[128,128]{1,0:T(8,128)(2,1)S(1)}, f32[128,128]{1,0:T(8,128)S(1)}, bf16[128,384]{1,0:T(8,128)(2,1)S(1)}) custom-call(bf16[256,256]{1,0:T(8,128)(2,1)S(1)} %add_add_fusion.lead_ref), custom_call_target="tpu_custom_call" | custom-call | tf_op jit(solution)/shard_map/factor/pallas_call | solution.py:95
  18.4 0.0 copy-start
  18.4 197.8 %all_to_all.5 = bf16[64,8,128,128]{3,2,1,0:T(8,128)(2,1)} all-to-all(bf16[64,8,128,128]{3,2,1,0:T(8,128)(2,1)} %bitcast.22), channel_id=1, replica_groups=mesh['group'=16,'row'=4,'col'=2] {'group','row'}, dimensions={0} | all-to-all | bytes 33554432 | tf_op jit(solution)/shard_map/all_to_all | solution.py:315
  216.2 0.0 copy-done
  216.2 5.0 %assemble.3 = (f32[40,128,256]{2,1,0:T(8,128)}, bf16[1280,256]{1,0:T(8,128)(2,1)S(1)}) custom-call(s32[512]{0:T(512)S(1)} %broadcast_select_fusion.target, s32[2]{0:T(128)S(1)} %pad_add_fusion.place, bf16[512,128,128]{2,1,0:T(8,128)(2,1)} %bitcast.19, bf16[40,128,256]{2,1,0:T(8,128)(2,1)S(1)} %bitcast.16, bf16[128,384]{1,0:T(8,128)(2,1)S(1)} %get-tuple-element.21.i1_ref, ...), custom_call_target="tpu_custom_call" | custom-call | flops 83886080 | bytes 4194304 | tf_op jit(solution)/shard_map/assemble/pallas_call | solution.py:197
  221.2 1.3 collective-permute-start.3
  222.5 6.4 %assemble.4 = (f32[40,128,256]{2,1,0:T(8,128)}, bf16[2560,256]{1,0:T(8,128)(2,1)S(1)}) custom-call(s32[512]{0:T(512)S(1)} %broadcast_select_fusion.target, s32[2]{0:T(128)S(1)} %pad_add_fusion.place, bf16[512,128,128]{2,1,0:T(8,128)(2,1)} %bitcast.20, bf16[40,128,256]{2,1,0:T(8,128)(2,1)S(1)} %bitcast.17, ...), custom_call_target="tpu_custom_call", output_to_operand_aliasing={{0}: (9, {})} | custom-call | flops 167772160 | bytes 8388608 | tf_op jit(solution)/shard_map/assemble/pallas_call | solution.py:197
  228.9 1.3 collective-permute-start.8
  230.3 11.7 %collective-permute-done.3.refs_0_ = bf16[1280,256]{1,0:T(8,128)(2,1)S(1)} collective-permute-done((bf16[1280,256]{1,0:T(8,128)(2,1)S(1)}, bf16[1280,256]{1,0:T(8,128)(2,1)S(1)}, u32[]{:S(2)}, u32[]{:S(2)}) %collective-permute-start.3) | collective-permute-done | bytes 655392 | tf_op jit(solution)/shard_map/ppermute | solution.py:359
  242.0 5.0 %assemble.5 = (f32[40,128,256]{2,1,0:T(8,128)}, bf16[1280,256]{1,0:T(8,128)(2,1)S(1)}) custom-call(s32[512]{0:T(512)S(1)} %broadcast_select_fusion.target, s32[2]{0:T(128)S(1)} %pad_add_fusion.place, bf16[512,128,128]{2,1,0:T(8,128)(2,1)} %bitcast.21, bf16[40,128,256]{2,1,0:T(8,128)(2,1)S(1)} %bitcast.18, ...), custom_call_target="tpu_custom_call", output_to_operand_aliasing={{0}: (9, {})} | custom-call | flops 83886080 | bytes 4194304 | tf_op jit(solution)/shard_map/assemble/pallas_call | solution.py:197
  247.0 1.3 collective-permute-start.5
  248.3 0.7 collective-permute-start.4
  249.0 29.7 %collective-permute-done.5 = bf16[256,256]{1,0:T(8,128)(2,1)S(1)} collective-permute-done((bf16[256,256]{1,0:T(8,128)(2,1)S(1)}, bf16[256,256]{1,0:T(8,128)(2,1)S(1)}, u32[]{:S(2)}, u32[]{:S(2)}) %collective-permute-start.5) | collective-permute-done | bytes 131104 | tf_op jit(solution)/shard_map/ppermute | solution.py:355
  278.7 0.0 collective-permute-done.4
  278.7 1.3 collective-permute-start.7
  280.0 1.3 collective-permute-start.6
  281.3 1.0 collective-permute-done.6
  282.3 0.0 collective-permute-done.8.refs_1_
  282.3 5.6 %update.2.refs_1_ = f32[40,128,256]{2,1,0:T(8,128)} custom-call(s32[2]{0:T(128)S(1)} %pad_add_fusion.place, bf16[256,256]{1,0:T(8,128)(2,1)S(1)} %add.28.p_hbm, bf16[1280,256]{1,0:T(8,128)(2,1)S(1)} %collective-permute-done.3.refs_0_, bf16[2560,256]{1,0:T(8,128)(2,1)S(1)} %collective-permute-done.8.refs_1_, ...), custom_call_target="tpu_custom_call", output_to_operand_aliasing={{}: (4, {})} | custom-call | flops 503316480 | bytes 9830400 | tf_op jit(solution)/shard_map/update/pallas_call | solution.py:274
  288.0 4.8 %collective-permute-done.7.refs_0_ = bf16[1280,256]{1,0:T(8,128)(2,1)S(1)} collective-permute-done((bf16[1280,256]{1,0:T(8,128)(2,1)S(1)}, bf16[1280,256]{1,0:T(8,128)(2,1)S(1)}, u32[]{:S(2)}, u32[]{:S(2)}) %collective-permute-start.7) | collective-permute-done | bytes 655392 | tf_op jit(solution)/shard_map/ppermute | solution.py:359
  292.7 3.7 %update.3 = f32[40,128,256]{2,1,0:T(8,128)} custom-call(s32[2]{0:T(128)S(1)} %pad_add_fusion.place, bf16[256,256]{1,0:T(8,128)(2,1)S(1)} %add.28.p_hbm, bf16[1280,256]{1,0:T(8,128)(2,1)S(1)} %collective-permute-done.7.refs_0_, f32[40,128,256]{2,1,0:T(8,128)} %update.2.refs_1_), custom_call_target="tpu_custom_call", output_to_operand_aliasing={{}: (3, {})} | custom-call | flops 167772160 | bytes 3276800 | tf_op jit(solution)/shard_map/update/pallas_call | solution.py:274
  (7 shorter events, 0.1 us)
Async XLA Ops:
  0.9 6.9 %collective-permute-start.1 = (bf16[256,256]{1,0:T(8,128)(2,1)S(1)}, bf16[256,256]{1,0:T(8,128)(2,1)S(1)}, u32[]{:S(2)}, u32[]{:S(2)}) collective-permute-start(bf16[256,256]{1,0:T(8,128)(2,1)S(1)} %slice_bitcast_fusion), channel_id=1, source_target_pairs={{0,4},{1,5},{8,12},{9,13},{16,20},{17,21},{24,28},{25,29},{32,36},... | collective-permute-start | bytes 393224 | tf_op jit(solution)/shard_map/ppermute | solution.py:306
  2.2 5.6 %collective-permute-start = (bf16[256,256]{1,0:T(8,128)(2,1)S(1)}, bf16[256,256]{1,0:T(8,128)(2,1)S(1)}, u32[]{:S(2)}, u32[]{:S(2)}) collective-permute-start(bf16[256,256]{1,0:T(8,128)(2,1)S(1)} %slice_bitcast_fusion), channel_id=1, source_target_pairs={{0,2},{1,3},{8,10},{9,11},{16,18},{17,19},{24,26},{25,27},{32,34},... | collective-permute-start | bytes 393224 | tf_op jit(solution)/shard_map/ppermute | solution.py:306
  2.9 4.9 %collective-permute-start.2 = (bf16[256,256]{1,0:T(8,128)(2,1)S(1)}, bf16[256,256]{1,0:T(8,128)(2,1)S(1)}, u32[]{:S(2)}, u32[]{:S(2)}) collective-permute-start(bf16[256,256]{1,0:T(8,128)(2,1)S(1)} %slice_bitcast_fusion), channel_id=1, source_target_pairs={{0,6},{1,7},{8,14},{9,15},{16,22},{17,23},{24,30},{25,31},{32,38},... | collective-permute-start | bytes 393224 | tf_op jit(solution)/shard_map/ppermute | solution.py:306
  18.4 197.8 %copy-start = (bf16[1,5120,256]{2,1,0:T(8,128)(2,1)S(1)}, bf16[1,5120,256]{2,1,0:T(8,128)(2,1)}, u32[]{:S(2)}) copy-start(bf16[1,5120,256]{2,1,0:T(8,128)(2,1)} %param.5) | copy-start | bytes 7864324
  221.2 20.8 %collective-permute-start.3 = (bf16[1280,256]{1,0:T(8,128)(2,1)S(1)}, bf16[1280,256]{1,0:T(8,128)(2,1)S(1)}, u32[]{:S(2)}, u32[]{:S(2)}) collective-permute-start(bf16[1280,256]{1,0:T(8,128)(2,1)S(1)} %get-tuple-element.27), channel_id=1, source_target_pairs={{0,1},{2,3},{4,5},{6,7},{8,9},{10,11},{12,13},{14,15},{16,17},{18,... | collective-permute-start | bytes 1966088 | tf_op jit(solution)/shard_map/ppermute | solution.py:359
  228.9 53.4 %collective-permute-start.8 = (bf16[2560,256]{1,0:T(8,128)(2,1)S(1)}, bf16[2560,256]{1,0:T(8,128)(2,1)S(1)}, u32[]{:S(2)}, u32[]{:S(2)}) collective-permute-start(bf16[2560,256]{1,0:T(8,128)(2,1)S(1)} %get-tuple-element.30), channel_id=1, source_target_pairs={{0,1},{2,3},{4,5},{6,7},{8,9},{10,11},{12,13},{14,15},{16,17},{18,... | collective-permute-start | bytes 3932168 | tf_op jit(solution)/shard_map/ppermute | solution.py:359
  247.0 31.7 %collective-permute-start.5 = (bf16[256,256]{1,0:T(8,128)(2,1)S(1)}, bf16[256,256]{1,0:T(8,128)(2,1)S(1)}, u32[]{:S(2)}, u32[]{:S(2)}) collective-permute-start(bf16[256,256]{1,0:T(8,128)(2,1)S(1)} %bitcast.24), channel_id=1, source_target_pairs={{0,5},{8,13},{16,21},{24,29},{32,37},{40,45},{48,53},{56,61},{64,6... | collective-permute-start | bytes 393224 | tf_op jit(solution)/shard_map/ppermute | solution.py:355
  248.3 30.4 %collective-permute-start.4 = (bf16[256,256]{1,0:T(8,128)(2,1)S(1)}, bf16[256,256]{1,0:T(8,128)(2,1)S(1)}, u32[]{:S(2)}, u32[]{:S(2)}) collective-permute-start(bf16[256,256]{1,0:T(8,128)(2,1)S(1)} %bitcast.25), channel_id=1, source_target_pairs={{0,1},{8,9},{16,17},{24,25},{32,33},{40,41},{48,49},{56,57},{64,65... | collective-permute-start | bytes 393224 | tf_op jit(solution)/shard_map/ppermute | solution.py:355
  278.7 14.0 %collective-permute-start.7 = (bf16[1280,256]{1,0:T(8,128)(2,1)S(1)}, bf16[1280,256]{1,0:T(8,128)(2,1)S(1)}, u32[]{:S(2)}, u32[]{:S(2)}) collective-permute-start(bf16[1280,256]{1,0:T(8,128)(2,1)S(1)} %get-tuple-element.35), channel_id=1, source_target_pairs={{0,1},{2,3},{4,5},{6,7},{8,9},{10,11},{12,13},{14,15},{16,17},{18,... | collective-permute-start | bytes 1966088 | tf_op jit(solution)/shard_map/ppermute | solution.py:359
  280.0 2.3 collective-permute-start.6

commit v5 on v4

--- a/solution.py
+++ b/solution.py
@@ -12,7 +12,7 @@
 CHAINS = 4
 DEPTH = 4
 BLOCK = 64
-PIVOTS = 4
+PIVOTS = 8
 EXACT = lax.Precision.HIGHEST
 VMEM = pl.BlockSpec(memory_space=pltpu.VMEM)
 

time: 297 us -> 295 us (level)
  no operation moved by 1% of the time
where the time goes in v5:
time: 295 us; the launch traced here: 294 us
  blocking collectives  198 us (67%)
  waiting for transfers between devices  49.3 us (17%)
  Pallas kernels  33 us (11%)
  starting transfers between devices  9.76 us (3%)
    all_to_all x1, blocking collectives, exchange(): lax.all_to_all(x, ('group', 'row'), split_axis=0, concat_axis=0, tiled=True)  198 us
    ppermute x2, waiting for transfers between devices, local(): near = [lax.ppermute(columns, ('row', 'col'), [(0, t)]) for t in (1, 5)]  29.7 us
    ppermute x3, waiting for transfers between devices, local(): halves.append(lax.ppermute(h, 'col', [(0, 1)]))  16.5 us
    pallas_call x3, Pallas kernels, assemble(): pl.pallas_call(functools.partial(assemble_kernel, rows, offset, start), g...  16.4 us
    pallas_call x2, Pallas kernels, update(): pl.pallas_call(functools.partial(update_kernel, pieces), grid_spec=pltpu....  9.35 us
    pallas_call x1, Pallas kernels, factor_lead(): pl.pallas_call(factor_kernel, out_shape=[square, wide, jax.ShapeDtypeStru...  7.2 us
  transfers between devices with their start and end apart: 9, of which 5 were waited for; matrix products, arithmetic and copies ran while one was open for 1% of the time, Pallas kernels for 6%

profile of v5, /device:TPU:14, one launch (start us, length us, event | category | flops | bytes accessed | tf_op | source)
XLA Modules:
  0.0 294.2 jit_solution(372530876116861152)
XLA Ops:
  0.0 0.9 slice_bitcast_fusion
  0.9 1.3 collective-permute-start.1
  2.2 0.7 collective-permute-start
  2.9 0.7 collective-permute-start.2
  3.6 0.8 copy.11
  4.3 0.1 lt.20
  4.4 0.1 iota_compare_fusion
  4.5 0.1 lt.23
  4.6 0.7 multiply_add_fusion
  5.4 0.1 copy.12
  5.4 0.1 add.23
  5.6 0.1 pad_add_fusion.place
  5.6 2.1 collective-permute-done.1
  7.8 0.0 collective-permute-done
  7.8 0.0 collective-permute-done.2
  7.8 0.9 add_add_fusion.lead_ref
  8.7 7.2 %factor.1 = (f32[128,128]{1,0:T(8,128)S(1)}, bf16[128,384]{1,0:T(8,128)(2,1)S(1)}, bf16[128,128]{1,0:T(8,128)(2,1)S(1)}, f32[128,128]{1,0:T(8,128)S(1)}, bf16[128,384]{1,0:T(8,128)(2,1)S(1)}) custom-call(bf16[256,256]{1,0:T(8,128)(2,1)S(1)} %add_add_fusion.lead_ref), custom_call_target="tpu_custom_call" | custom-call | tf_op jit(solution)/shard_map/factor/pallas_call | solution.py:95
  15.9 0.0 copy-start
  15.9 197.8 %all_to_all.5 = bf16[64,8,128,128]{3,2,1,0:T(8,128)(2,1)} all-to-all(bf16[64,8,128,128]{3,2,1,0:T(8,128)(2,1)} %bitcast.22), channel_id=1, replica_groups=mesh['group'=16,'row'=4,'col'=2] {'group','row'}, dimensions={0} | all-to-all | bytes 33554432 | tf_op jit(solution)/shard_map/all_to_all | solution.py:315
  213.7 0.0 copy-done
  213.7 5.0 %assemble.3 = (f32[40,128,256]{2,1,0:T(8,128)}, bf16[1280,256]{1,0:T(8,128)(2,1)S(1)}) custom-call(s32[512]{0:T(512)S(1)} %broadcast_select_fusion.target, s32[2]{0:T(128)S(1)} %pad_add_fusion.place, bf16[512,128,128]{2,1,0:T(8,128)(2,1)} %bitcast.19, bf16[40,128,256]{2,1,0:T(8,128)(2,1)S(1)} %bitcast.16, bf16[128,384]{1,0:T(8,128)(2,1)S(1)} %get-tuple-element.21.i1_ref, ...), custom_call_target="tpu_custom_call" | custom-call | flops 83886080 | bytes 4194304 | tf_op jit(solution)/shard_map/assemble/pallas_call | solution.py:197
  218.7 1.3 collective-permute-start.3
  220.0 6.4 %assemble.4 = (f32[40,128,256]{2,1,0:T(8,128)}, bf16[2560,256]{1,0:T(8,128)(2,1)S(1)}) custom-call(s32[512]{0:T(512)S(1)} %broadcast_select_fusion.target, s32[2]{0:T(128)S(1)} %pad_add_fusion.place, bf16[512,128,128]{2,1,0:T(8,128)(2,1)} %bitcast.20, bf16[40,128,256]{2,1,0:T(8,128)(2,1)S(1)} %bitcast.17, ...), custom_call_target="tpu_custom_call", output_to_operand_aliasing={{0}: (9, {})} | custom-call | flops 167772160 | bytes 8388608 | tf_op jit(solution)/shard_map/assemble/pallas_call | solution.py:197
  226.5 1.3 collective-permute-start.8
  227.8 11.7 %collective-permute-done.3.refs_0_ = bf16[1280,256]{1,0:T(8,128)(2,1)S(1)} collective-permute-done((bf16[1280,256]{1,0:T(8,128)(2,1)S(1)}, bf16[1280,256]{1,0:T(8,128)(2,1)S(1)}, u32[]{:S(2)}, u32[]{:S(2)}) %collective-permute-start.3) | collective-permute-done | bytes 655392 | tf_op jit(solution)/shard_map/ppermute | solution.py:359
  239.5 5.0 %assemble.5 = (f32[40,128,256]{2,1,0:T(8,128)}, bf16[1280,256]{1,0:T(8,128)(2,1)S(1)}) custom-call(s32[512]{0:T(512)S(1)} %broadcast_select_fusion.target, s32[2]{0:T(128)S(1)} %pad_add_fusion.place, bf16[512,128,128]{2,1,0:T(8,128)(2,1)} %bitcast.21, bf16[40,128,256]{2,1,0:T(8,128)(2,1)S(1)} %bitcast.18, ...), custom_call_target="tpu_custom_call", output_to_operand_aliasing={{0}: (9, {})} | custom-call | flops 83886080 | bytes 4194304 | tf_op jit(solution)/shard_map/assemble/pallas_call | solution.py:197
  244.5 1.3 collective-permute-start.5
  245.8 0.7 collective-permute-start.4
  246.5 29.7 %collective-permute-done.5 = bf16[256,256]{1,0:T(8,128)(2,1)S(1)} collective-permute-done((bf16[256,256]{1,0:T(8,128)(2,1)S(1)}, bf16[256,256]{1,0:T(8,128)(2,1)S(1)}, u32[]{:S(2)}, u32[]{:S(2)}) %collective-permute-start.5) | collective-permute-done | bytes 131104 | tf_op jit(solution)/shard_map/ppermute | solution.py:355
  276.2 0.0 collective-permute-done.4
  276.3 1.3 collective-permute-start.7
  277.6 1.3 collective-permute-start.6
  278.9 1.0 collective-permute-done.6
  279.9 0.0 collective-permute-done.8.refs_1_
  279.9 5.6 %update.2.refs_1_ = f32[40,128,256]{2,1,0:T(8,128)} custom-call(s32[2]{0:T(128)S(1)} %pad_add_fusion.place, bf16[256,256]{1,0:T(8,128)(2,1)S(1)} %add.28.p_hbm, bf16[1280,256]{1,0:T(8,128)(2,1)S(1)} %collective-permute-done.3.refs_0_, bf16[2560,256]{1,0:T(8,128)(2,1)S(1)} %collective-permute-done.8.refs_1_, ...), custom_call_target="tpu_custom_call", output_to_operand_aliasing={{}: (4, {})} | custom-call | flops 503316480 | bytes 9830400 | tf_op jit(solution)/shard_map/update/pallas_call | solution.py:274
  285.5 4.8 %collective-permute-done.7.refs_0_ = bf16[1280,256]{1,0:T(8,128)(2,1)S(1)} collective-permute-done((bf16[1280,256]{1,0:T(8,128)(2,1)S(1)}, bf16[1280,256]{1,0:T(8,128)(2,1)S(1)}, u32[]{:S(2)}, u32[]{:S(2)}) %collective-permute-start.7) | collective-permute-done | bytes 655392 | tf_op jit(solution)/shard_map/ppermute | solution.py:359
  290.3 3.7 %update.3 = f32[40,128,256]{2,1,0:T(8,128)} custom-call(s32[2]{0:T(128)S(1)} %pad_add_fusion.place, bf16[256,256]{1,0:T(8,128)(2,1)S(1)} %add.28.p_hbm, bf16[1280,256]{1,0:T(8,128)(2,1)S(1)} %collective-permute-done.7.refs_0_, f32[40,128,256]{2,1,0:T(8,128)} %update.2.refs_1_), custom_call_target="tpu_custom_call", output_to_operand_aliasing={{}: (3, {})} | custom-call | flops 167772160 | bytes 3276800 | tf_op jit(solution)/shard_map/update/pallas_call | solution.py:274
  (7 shorter events, 0.1 us)
Async XLA Ops:
  0.9 6.9 %collective-permute-start.1 = (bf16[256,256]{1,0:T(8,128)(2,1)S(1)}, bf16[256,256]{1,0:T(8,128)(2,1)S(1)}, u32[]{:S(2)}, u32[]{:S(2)}) collective-permute-start(bf16[256,256]{1,0:T(8,128)(2,1)S(1)} %slice_bitcast_fusion), channel_id=1, source_target_pairs={{0,4},{1,5},{8,12},{9,13},{16,20},{17,21},{24,28},{25,29},{32,36},... | collective-permute-start | bytes 393224 | tf_op jit(solution)/shard_map/ppermute | solution.py:306
  2.2 5.6 %collective-permute-start = (bf16[256,256]{1,0:T(8,128)(2,1)S(1)}, bf16[256,256]{1,0:T(8,128)(2,1)S(1)}, u32[]{:S(2)}, u32[]{:S(2)}) collective-permute-start(bf16[256,256]{1,0:T(8,128)(2,1)S(1)} %slice_bitcast_fusion), channel_id=1, source_target_pairs={{0,2},{1,3},{8,10},{9,11},{16,18},{17,19},{24,26},{25,27},{32,34},... | collective-permute-start | bytes 393224 | tf_op jit(solution)/shard_map/ppermute | solution.py:306
  2.9 4.9 %collective-permute-start.2 = (bf16[256,256]{1,0:T(8,128)(2,1)S(1)}, bf16[256,256]{1,0:T(8,128)(2,1)S(1)}, u32[]{:S(2)}, u32[]{:S(2)}) collective-permute-start(bf16[256,256]{1,0:T(8,128)(2,1)S(1)} %slice_bitcast_fusion), channel_id=1, source_target_pairs={{0,6},{1,7},{8,14},{9,15},{16,22},{17,23},{24,30},{25,31},{32,38},... | collective-permute-start | bytes 393224 | tf_op jit(solution)/shard_map/ppermute | solution.py:306
  15.9 197.8 %copy-start = (bf16[1,5120,256]{2,1,0:T(8,128)(2,1)S(1)}, bf16[1,5120,256]{2,1,0:T(8,128)(2,1)}, u32[]{:S(2)}) copy-start(bf16[1,5120,256]{2,1,0:T(8,128)(2,1)} %param.5) | copy-start | bytes 7864324
  218.7 20.8 %collective-permute-start.3 = (bf16[1280,256]{1,0:T(8,128)(2,1)S(1)}, bf16[1280,256]{1,0:T(8,128)(2,1)S(1)}, u32[]{:S(2)}, u32[]{:S(2)}) collective-permute-start(bf16[1280,256]{1,0:T(8,128)(2,1)S(1)} %get-tuple-element.27), channel_id=1, source_target_pairs={{0,1},{2,3},{4,5},{6,7},{8,9},{10,11},{12,13},{14,15},{16,17},{18,... | collective-permute-start | bytes 1966088 | tf_op jit(solution)/shard_map/ppermute | solution.py:359
  226.5 53.4 %collective-permute-start.8 = (bf16[2560,256]{1,0:T(8,128)(2,1)S(1)}, bf16[2560,256]{1,0:T(8,128)(2,1)S(1)}, u32[]{:S(2)}, u32[]{:S(2)}) collective-permute-start(bf16[2560,256]{1,0:T(8,128)(2,1)S(1)} %get-tuple-element.30), channel_id=1, source_target_pairs={{0,1},{2,3},{4,5},{6,7},{8,9},{10,11},{12,13},{14,15},{16,17},{18,... | collective-permute-start | bytes 3932168 | tf_op jit(solution)/shard_map/ppermute | solution.py:359
  244.5 31.7 %collective-permute-start.5 = (bf16[256,256]{1,0:T(8,128)(2,1)S(1)}, bf16[256,256]{1,0:T(8,128)(2,1)S(1)}, u32[]{:S(2)}, u32[]{:S(2)}) collective-permute-start(bf16[256,256]{1,0:T(8,128)(2,1)S(1)} %bitcast.24), channel_id=1, source_target_pairs={{0,5},{8,13},{16,21},{24,29},{32,37},{40,45},{48,53},{56,61},{64,6... | collective-permute-start | bytes 393224 | tf_op jit(solution)/shard_map/ppermute | solution.py:355
  245.8 30.4 %collective-permute-start.4 = (bf16[256,256]{1,0:T(8,128)(2,1)S(1)}, bf16[256,256]{1,0:T(8,128)(2,1)S(1)}, u32[]{:S(2)}, u32[]{:S(2)}) collective-permute-start(bf16[256,256]{1,0:T(8,128)(2,1)S(1)} %bitcast.25), channel_id=1, source_target_pairs={{0,1},{8,9},{16,17},{24,25},{32,33},{40,41},{48,49},{56,57},{64,65... | collective-permute-start | bytes 393224 | tf_op jit(solution)/shard_map/ppermute | solution.py:355
  276.3 14.0 %collective-permute-start.7 = (bf16[1280,256]{1,0:T(8,128)(2,1)S(1)}, bf16[1280,256]{1,0:T(8,128)(2,1)S(1)}, u32[]{:S(2)}, u32[]{:S(2)}) collective-permute-start(bf16[1280,256]{1,0:T(8,128)(2,1)S(1)} %get-tuple-element.35), channel_id=1, source_target_pairs={{0,1},{2,3},{4,5},{6,7},{8,9},{10,11},{12,13},{14,15},{16,17},{18,... | collective-permute-start | bytes 1966088 | tf_op jit(solution)/shard_map/ppermute | solution.py:359
  277.6 2.3 collective-permute-start.6

commit v6 on v5

--- a/solution.py
+++ b/solution.py
@@ -230,7 +230,7 @@
     halves = refs[:n]
     out_hbm, p_ref, f_ref, h_ref, p_sem, f_sem, h_sem, o_sem = refs[n + 1 :]
     tiles, first = f_ref.shape[0], pieces[0][0]
-    batch = 8
+    batch = 20
 
     @pl.when(place[1] == 1)
     def _():
@@ -269,7 +269,7 @@
 def update(place, front, halves, pieces, columns):
     tiles = front.shape[0]
     rows = sum(r for _, r in pieces)
-    steps = len(pieces) * (tiles // 8)
+    steps = len(pieces) * (tiles // 20)
     anywhere = pl.BlockSpec(memory_space=pl.ANY)
     return pl.pallas_call(
         functools.partial(update_kernel, pieces),

time: 295 us -> 294 us (level)
  no operation moved by 1% of the time
where the time goes in v6:
time: 294 us
  blocking collectives  198 us (67%)
  waiting for transfers between devices  50.1 us (17%)
  Pallas kernels  31.9 us (11%)
  starting transfers between devices  9.76 us (3%)
    all_to_all x1, blocking collectives, exchange(): lax.all_to_all(x, ('group', 'row'), split_axis=0, concat_axis=0, tiled=True)  198 us
    ppermute x2, waiting for transfers between devices, local(): near = [lax.ppermute(columns, ('row', 'col'), [(0, t)]) for t in (1, 5)]  29.7 us
    ppermute x3, waiting for transfers between devices, local(): halves.append(lax.ppermute(h, 'col', [(0, 1)]))  17.2 us
    pallas_call x3, Pallas kernels, assemble(): pl.pallas_call(functools.partial(assemble_kernel, rows, offset, start), g...  16.4 us
    pallas_call x2, Pallas kernels, update(): pl.pallas_call(functools.partial(update_kernel, pieces), grid_spec=pltpu....  8.24 us
    pallas_call x1, Pallas kernels, factor_lead(): pl.pallas_call(factor_kernel, out_shape=[square, wide, jax.ShapeDtypeStru...  7.2 us
  transfers between devices with their start and end apart: 9, of which 5 were waited for; matrix products, arithmetic and copies ran while one was open for 1% of the time, Pallas kernels for 6%

profile of v6, /device:TPU:14, one launch (start us, length us, event | category | flops | bytes accessed | tf_op | source)
XLA Modules:
  0.0 293.8 jit_solution(9742488074197660790)
XLA Ops:
  0.0 0.9 slice_bitcast_fusion
  0.9 1.3 collective-permute-start.1
  2.2 0.7 collective-permute-start
  2.9 0.7 collective-permute-start.2
  3.6 0.8 copy.11
  4.3 0.1 lt.20
  4.4 0.1 iota_compare_fusion
  4.5 0.1 lt.23
  4.6 0.7 multiply_add_fusion
  5.4 0.1 copy.12
  5.4 0.1 add.23
  5.6 0.1 pad_add_fusion.place
  5.6 2.1 collective-permute-done.1
  7.8 0.0 collective-permute-done
  7.8 0.0 collective-permute-done.2
  7.8 0.9 add_add_fusion.lead_ref
  8.7 7.2 %factor.1 = (f32[128,128]{1,0:T(8,128)S(1)}, bf16[128,384]{1,0:T(8,128)(2,1)S(1)}, bf16[128,128]{1,0:T(8,128)(2,1)S(1)}, f32[128,128]{1,0:T(8,128)S(1)}, bf16[128,384]{1,0:T(8,128)(2,1)S(1)}) custom-call(bf16[256,256]{1,0:T(8,128)(2,1)S(1)} %add_add_fusion.lead_ref), custom_call_target="tpu_custom_call" | custom-call | tf_op jit(solution)/shard_map/factor/pallas_call | solution.py:95
  15.9 0.0 copy-start
  15.9 197.8 %all_to_all.5 = bf16[64,8,128,128]{3,2,1,0:T(8,128)(2,1)} all-to-all(bf16[64,8,128,128]{3,2,1,0:T(8,128)(2,1)} %bitcast.22), channel_id=1, replica_groups=mesh['group'=16,'row'=4,'col'=2] {'group','row'}, dimensions={0} | all-to-all | bytes 33554432 | tf_op jit(solution)/shard_map/all_to_all | solution.py:315
  213.7 0.0 copy-done
  213.7 5.0 %assemble.3 = (f32[40,128,256]{2,1,0:T(8,128)}, bf16[1280,256]{1,0:T(8,128)(2,1)S(1)}) custom-call(s32[512]{0:T(512)S(1)} %broadcast_select_fusion.target, s32[2]{0:T(128)S(1)} %pad_add_fusion.place, bf16[512,128,128]{2,1,0:T(8,128)(2,1)} %bitcast.19, bf16[40,128,256]{2,1,0:T(8,128)(2,1)S(1)} %bitcast.16, bf16[128,384]{1,0:T(8,128)(2,1)S(1)} %get-tuple-element.21.i1_ref, ...), custom_call_target="tpu_custom_call" | custom-call | flops 83886080 | bytes 4194304 | tf_op jit(solution)/shard_map/assemble/pallas_call | solution.py:197
  218.7 1.3 collective-permute-start.3
  220.0 6.4 %assemble.4 = (f32[40,128,256]{2,1,0:T(8,128)}, bf16[2560,256]{1,0:T(8,128)(2,1)S(1)}) custom-call(s32[512]{0:T(512)S(1)} %broadcast_select_fusion.target, s32[2]{0:T(128)S(1)} %pad_add_fusion.place, bf16[512,128,128]{2,1,0:T(8,128)(2,1)} %bitcast.20, bf16[40,128,256]{2,1,0:T(8,128)(2,1)S(1)} %bitcast.17, ...), custom_call_target="tpu_custom_call", output_to_operand_aliasing={{0}: (9, {})} | custom-call | flops 167772160 | bytes 8388608 | tf_op jit(solution)/shard_map/assemble/pallas_call | solution.py:197
  226.5 1.3 collective-permute-start.8
  227.8 11.7 %collective-permute-done.3.refs_0_ = bf16[1280,256]{1,0:T(8,128)(2,1)S(1)} collective-permute-done((bf16[1280,256]{1,0:T(8,128)(2,1)S(1)}, bf16[1280,256]{1,0:T(8,128)(2,1)S(1)}, u32[]{:S(2)}, u32[]{:S(2)}) %collective-permute-start.3) | collective-permute-done | bytes 655392 | tf_op jit(solution)/shard_map/ppermute | solution.py:359
  239.5 5.0 %assemble.5 = (f32[40,128,256]{2,1,0:T(8,128)}, bf16[1280,256]{1,0:T(8,128)(2,1)S(1)}) custom-call(s32[512]{0:T(512)S(1)} %broadcast_select_fusion.target, s32[2]{0:T(128)S(1)} %pad_add_fusion.place, bf16[512,128,128]{2,1,0:T(8,128)(2,1)} %bitcast.21, bf16[40,128,256]{2,1,0:T(8,128)(2,1)S(1)} %bitcast.18, ...), custom_call_target="tpu_custom_call", output_to_operand_aliasing={{0}: (9, {})} | custom-call | flops 83886080 | bytes 4194304 | tf_op jit(solution)/shard_map/assemble/pallas_call | solution.py:197
  244.5 1.3 collective-permute-start.5
  245.8 0.7 collective-permute-start.4
  246.5 29.7 %collective-permute-done.5 = bf16[256,256]{1,0:T(8,128)(2,1)S(1)} collective-permute-done((bf16[256,256]{1,0:T(8,128)(2,1)S(1)}, bf16[256,256]{1,0:T(8,128)(2,1)S(1)}, u32[]{:S(2)}, u32[]{:S(2)}) %collective-permute-start.5) | collective-permute-done | bytes 131104 | tf_op jit(solution)/shard_map/ppermute | solution.py:355
  276.2 0.0 collective-permute-done.4
  276.3 1.3 collective-permute-start.7
  277.6 1.3 collective-permute-start.6
  278.9 1.0 collective-permute-done.6
  279.9 0.0 collective-permute-done.8.refs_1_
  279.9 4.8 %update.2.refs_1_ = f32[40,128,256]{2,1,0:T(8,128)} custom-call(s32[2]{0:T(128)S(1)} %pad_add_fusion.place, bf16[256,256]{1,0:T(8,128)(2,1)S(1)} %add.28.p_hbm, bf16[1280,256]{1,0:T(8,128)(2,1)S(1)} %collective-permute-done.3.refs_0_, bf16[2560,256]{1,0:T(8,128)(2,1)S(1)} %collective-permute-done.8.refs_1_, ...), custom_call_target="tpu_custom_call", output_to_operand_aliasing={{}: (4, {})} | custom-call | flops 503316480 | bytes 9830400 | tf_op jit(solution)/shard_map/update/pallas_call | solution.py:274
  284.7 5.5 %collective-permute-done.7.refs_0_ = bf16[1280,256]{1,0:T(8,128)(2,1)S(1)} collective-permute-done((bf16[1280,256]{1,0:T(8,128)(2,1)S(1)}, bf16[1280,256]{1,0:T(8,128)(2,1)S(1)}, u32[]{:S(2)}, u32[]{:S(2)}) %collective-permute-start.7) | collective-permute-done | bytes 655392 | tf_op jit(solution)/shard_map/ppermute | solution.py:359
  290.3 3.4 %update.3 = f32[40,128,256]{2,1,0:T(8,128)} custom-call(s32[2]{0:T(128)S(1)} %pad_add_fusion.place, bf16[256,256]{1,0:T(8,128)(2,1)S(1)} %add.28.p_hbm, bf16[1280,256]{1,0:T(8,128)(2,1)S(1)} %collective-permute-done.7.refs_0_, f32[40,128,256]{2,1,0:T(8,128)} %update.2.refs_1_), custom_call_target="tpu_custom_call", output_to_operand_aliasing={{}: (3, {})} | custom-call | flops 167772160 | bytes 3276800 | tf_op jit(solution)/shard_map/update/pallas_call | solution.py:274
  (7 shorter events, 0.1 us)
Async XLA Ops:
  0.9 6.9 %collective-permute-start.1 = (bf16[256,256]{1,0:T(8,128)(2,1)S(1)}, bf16[256,256]{1,0:T(8,128)(2,1)S(1)}, u32[]{:S(2)}, u32[]{:S(2)}) collective-permute-start(bf16[256,256]{1,0:T(8,128)(2,1)S(1)} %slice_bitcast_fusion), channel_id=1, source_target_pairs={{0,4},{1,5},{8,12},{9,13},{16,20},{17,21},{24,28},{25,29},{32,36},... | collective-permute-start | bytes 393224 | tf_op jit(solution)/shard_map/ppermute | solution.py:306
  2.2 5.6 %collective-permute-start = (bf16[256,256]{1,0:T(8,128)(2,1)S(1)}, bf16[256,256]{1,0:T(8,128)(2,1)S(1)}, u32[]{:S(2)}, u32[]{:S(2)}) collective-permute-start(bf16[256,256]{1,0:T(8,128)(2,1)S(1)} %slice_bitcast_fusion), channel_id=1, source_target_pairs={{0,2},{1,3},{8,10},{9,11},{16,18},{17,19},{24,26},{25,27},{32,34},... | collective-permute-start | bytes 393224 | tf_op jit(solution)/shard_map/ppermute | solution.py:306
  2.9 4.9 %collective-permute-start.2 = (bf16[256,256]{1,0:T(8,128)(2,1)S(1)}, bf16[256,256]{1,0:T(8,128)(2,1)S(1)}, u32[]{:S(2)}, u32[]{:S(2)}) collective-permute-start(bf16[256,256]{1,0:T(8,128)(2,1)S(1)} %slice_bitcast_fusion), channel_id=1, source_target_pairs={{0,6},{1,7},{8,14},{9,15},{16,22},{17,23},{24,30},{25,31},{32,38},... | collective-permute-start | bytes 393224 | tf_op jit(solution)/shard_map/ppermute | solution.py:306
  15.9 197.8 %copy-start = (bf16[1,5120,256]{2,1,0:T(8,128)(2,1)S(1)}, bf16[1,5120,256]{2,1,0:T(8,128)(2,1)}, u32[]{:S(2)}) copy-start(bf16[1,5120,256]{2,1,0:T(8,128)(2,1)} %param.5) | copy-start | bytes 7864324
  218.7 20.8 %collective-permute-start.3 = (bf16[1280,256]{1,0:T(8,128)(2,1)S(1)}, bf16[1280,256]{1,0:T(8,128)(2,1)S(1)}, u32[]{:S(2)}, u32[]{:S(2)}) collective-permute-start(bf16[1280,256]{1,0:T(8,128)(2,1)S(1)} %get-tuple-element.27), channel_id=1, source_target_pairs={{0,1},{2,3},{4,5},{6,7},{8,9},{10,11},{12,13},{14,15},{16,17},{18,... | collective-permute-start | bytes 1966088 | tf_op jit(solution)/shard_map/ppermute | solution.py:359
  226.5 53.4 %collective-permute-start.8 = (bf16[2560,256]{1,0:T(8,128)(2,1)S(1)}, bf16[2560,256]{1,0:T(8,128)(2,1)S(1)}, u32[]{:S(2)}, u32[]{:S(2)}) collective-permute-start(bf16[2560,256]{1,0:T(8,128)(2,1)S(1)} %get-tuple-element.30), channel_id=1, source_target_pairs={{0,1},{2,3},{4,5},{6,7},{8,9},{10,11},{12,13},{14,15},{16,17},{18,... | collective-permute-start | bytes 3932168 | tf_op jit(solution)/shard_map/ppermute | solution.py:359
  244.5 31.7 %collective-permute-start.5 = (bf16[256,256]{1,0:T(8,128)(2,1)S(1)}, bf16[256,256]{1,0:T(8,128)(2,1)S(1)}, u32[]{:S(2)}, u32[]{:S(2)}) collective-permute-start(bf16[256,256]{1,0:T(8,128)(2,1)S(1)} %bitcast.24), channel_id=1, source_target_pairs={{0,5},{8,13},{16,21},{24,29},{32,37},{40,45},{48,53},{56,61},{64,6... | collective-permute-start | bytes 393224 | tf_op jit(solution)/shard_map/ppermute | solution.py:355
  245.8 30.4 %collective-permute-start.4 = (bf16[256,256]{1,0:T(8,128)(2,1)S(1)}, bf16[256,256]{1,0:T(8,128)(2,1)S(1)}, u32[]{:S(2)}, u32[]{:S(2)}) collective-permute-start(bf16[256,256]{1,0:T(8,128)(2,1)S(1)} %bitcast.25), channel_id=1, source_target_pairs={{0,1},{8,9},{16,17},{24,25},{32,33},{40,41},{48,49},{56,57},{64,65... | collective-permute-start | bytes 393224 | tf_op jit(solution)/shard_map/ppermute | solution.py:355
  276.3 14.0 %collective-permute-start.7 = (bf16[1280,256]{1,0:T(8,128)(2,1)S(1)}, bf16[1280,256]{1,0:T(8,128)(2,1)S(1)}, u32[]{:S(2)}, u32[]{:S(2)}) collective-permute-start(bf16[1280,256]{1,0:T(8,128)(2,1)S(1)} %get-tuple-element.35), channel_id=1, source_target_pairs={{0,1},{2,3},{4,5},{6,7},{8,9},{10,11},{12,13},{14,15},{16,17},{18,... | collective-permute-start | bytes 1966088 | tf_op jit(solution)/shard_map/ppermute | solution.py:359
  277.6 2.3 collective-permute-start.6
